TPU v7x, 128 devices: a whole 4x4x4 slice. The times are simulated.
128 devices in a mesh: queue: 4 (over x_hi, core), ctx: 32 (over x_lo, z, y).
Axes of the slice: x: 4 (x_hi: 2, x_lo: 2; x = x_hi * 2 + x_lo), y: 4, z: 4, core: 2. Of those that a mesh axis runs over, the one named last changes fastest.
Arguments:
- queries: bfloat16 [4, 2048, 32, 128], P('queue', 'ctx'), may hold values from -110 to 110, as said below
- keys: bfloat16 [4, 2048, 32, 128], P('queue', 'ctx'), may hold values from -9 to 9, as said below
- values: bfloat16 [4, 2048, 32, 128], P('queue', 'ctx'), may hold values from -6 to 6
- gate_table: float32 [8, 32, 128], replicated, may hold values from 0.5 to 2
- noise_level: int32 [4], replicated, may hold values from 0 to 7, as said below
- stretch_order: int32 [4], replicated, may hold values from 0 to 3, each once
- block_mask: int32 [4, 4], replicated, may hold values from 0 to 1, as said below
Outputs:
- attended: bfloat16 [4, 2048, 32, 128], P('queue', 'ctx')
Inputs may be any that keep to these rules, and one draw needn't show every extreme that they name: queries follow a standard normal law clipped at 4.5, some rows a multiple of up to 24 of a key of the same stretch. keys follow a standard normal law clipped at 4.5, rows scaled by up to 2. `noise_level`: the stretches have pairwise distinct noise levels; level 0 and level 7 are always among them. block_mask[p, p] = 1 and block_mask[p, p - 1] = 1; block_mask[p, q] = 0 for q > p; entries with q < p - 1 are 0 or 1.
All inputs are finite; a program needn't handle non-finite values.
Results may differ from a plain program's by a relative error of at most 0.01.
Values may be sent and summed in bfloat16 or wider, within the bound.
No kernel may reach another device: no remote copies, remote signals or barrier semaphores. Data moves between devices by JAX's collectives and lax.ppermute only.
A program may use at most 192 MiB of HBM per device.

v0:
```python
import jax
import jax.numpy as jnp
from jax import lax
from jax.sharding import PartitionSpec as P


def flash_update(running, query_four, key_rows, value_rows, factor):
    row_max, total, mixed = running
    scores = (
        jnp.einsum("cthd,shd->cths", query_four, key_rows, preferred_element_type=jnp.float32)
        * factor
    )
    new_max = jnp.maximum(row_max, jnp.max(scores, axis=-1))
    rescale = jnp.exp(row_max - new_max)
    weights = jnp.exp(scores - new_max[..., None])
    total = total * rescale + jnp.sum(weights, axis=-1)
    mixed = mixed * rescale[..., None] + jnp.einsum(
        "cths,shd->cthd",
        weights.astype(jnp.bfloat16),
        value_rows,
        preferred_element_type=jnp.float32,
    )
    return (new_max, total, mixed)


def block_size(row_count):
    span_rows = row_count
    while span_rows > 512 and span_rows % 2 == 0:
        span_rows = span_rows // 2
    return span_rows


def combine_sources(source_max, source_total, source_mixed, usable):
    masked_max = jnp.where(usable > 0.5, source_max, -1e30)
    best = jnp.max(masked_max, axis=0)
    scales = jnp.exp(masked_max - best[None]) * usable
    final_total = jnp.sum(scales * source_total, axis=0)
    final_mixed = jnp.sum(scales[..., None] * source_mixed, axis=0)
    return (final_total, final_mixed)


def finish_tokens(row_max, total, mixed, allowed, self_hot, gate_rows):
    source_max, source_total, source_mixed = (
        lax.all_to_all(row_max, "queue", split_axis=0, concat_axis=0, tiled=True),
        lax.all_to_all(total, "queue", split_axis=0, concat_axis=0, tiled=True),
        lax.all_to_all(mixed, "queue", split_axis=0, concat_axis=0, tiled=True),
    )
    usable = jnp.dot(self_hot, allowed, precision=lax.Precision.HIGHEST)[:, None, None]
    final_total, final_mixed = combine_sources(source_max, source_total, source_mixed, usable)
    result = final_mixed / final_total[..., None] * gate_rows[None]
    return result.astype(jnp.bfloat16)[None]


def shards(queries, keys, values, gate_table, noise_level, stretch_order, block_mask):
    count = lax.axis_size("queue")
    stretch_index = lax.axis_index("queue")
    tok_rows = queries.shape[1]
    head_count = queries.shape[2]
    head_size = queries.shape[3]
    factor = 1.0 / head_size**0.5
    stretch_ids = jnp.arange(count, dtype=jnp.int32)
    order_hot = (stretch_order[:, None] == stretch_ids[None, :]).astype(jnp.float32)
    allowed = jnp.dot(
        jnp.dot(order_hot, block_mask.astype(jnp.float32), precision=lax.Precision.HIGHEST),
        order_hot.T,
        precision=lax.Precision.HIGHEST,
    )
    self_hot = (stretch_ids == stretch_index).astype(jnp.float32)
    my_level = jnp.sum(self_hot * noise_level.astype(jnp.float32))
    level_hot = (jnp.arange(gate_table.shape[0], dtype=jnp.float32) == my_level).astype(jnp.float32)
    gate_rows = jnp.einsum("l,lhd->hd", level_hot, gate_table, precision=lax.Precision.HIGHEST)
    query_local = queries[0]
    gathered = lax.all_gather(query_local, "queue", axis=0, tiled=True)
    query_four = gathered.reshape(count, tok_rows, head_count, head_size)
    paired = jnp.stack([keys[0], values[0]])
    initial = (
        jnp.full((count, tok_rows, head_count), -1e30, jnp.float32),
        jnp.zeros((count, tok_rows, head_count), jnp.float32),
        jnp.zeros((count, tok_rows, head_count, head_size), jnp.float32),
    )
    running = initial
    shard_rows = lax.all_gather(paired, "ctx", axis=1, tiled=True)
    row_count = shard_rows.shape[1]
    span_rows = block_size(row_count)
    for block_id in range(row_count // span_rows):
        key_rows = shard_rows[0, block_id * span_rows : (block_id + 1) * span_rows]
        value_rows = shard_rows[1, block_id * span_rows : (block_id + 1) * span_rows]
        running = flash_update(running, query_four, key_rows, value_rows, factor)
    row_max, total, mixed = running
    return finish_tokens(row_max, total, mixed, allowed, self_hot, gate_rows)


def solution(mesh):
    return jax.shard_map(
        shards,
        mesh=mesh,
        in_specs=(
            P("queue", "ctx", None, None),
            P("queue", "ctx", None, None),
            P("queue", "ctx", None, None),
            P(),
            P(),
            P(),
            P(),
        ),
        out_specs=P("queue", "ctx", None, None),
        check_vma=False,
    )
```

profile of v0, /device:TPU:1, one launch (start us, length us, event | category | flops | bytes accessed | tf_op | source)
XLA Modules:
  0.0 635.6 jit_solution(12880069765388599863)
XLA Ops:
  8.6 1.2 copy.40
  10.9 28.4 %all-gather.6.cloned.1.call-done = bf16[1,256,32,128]{3,2,0,1:T(8,128)(2,1)} async-done(((bf16[1,64,32,128]{3,2,0,1:T(8,128)(2,1)}), bf16[1,256,32,128]{3,2,0,1:T(8,128)(2,1)}) %all-gather.6.cloned.1.call-update) | async-done | bytes 2097168 | tf_op jit(solution)/shard_map/all_gather | solution.py:73
  39.3 365.6 %all-gather.4.cloned.1.call-done = bf16[2,2048,32,128]{3,1,2,0:T(8,128)(2,1)} async-done(((bf16[2,64,32,128]{3,1,2,0:T(8,128)(2,1)}), bf16[2,2048,32,128]{3,1,2,0:T(8,128)(2,1)}) %all-gather.4.cloned.1.call-update) | async-done | bytes 33554448 | tf_op jit(solution)/shard_map/all_gather | solution.py:82
  404.9 11.0 %fusion.18 = f32[32,512,256]{1,2,0} fusion(bf16[2,2048,32,128]{3,1,2,0:T(8,128)(2,1)} %all-gather.4.cloned.1.call-done, bf16[1,256,32,128]{3,2,0,1:T(8,128)(2,1)} %all-gather.6.cloned.1.call-done), kind=kOutput, calls=%fused_computation.33 | convolution fusion | flops 1073741824 | bytes 23068672
  415.9 10.3 %fusion.19 = f32[32,512,256]{1,2,0} fusion(bf16[2,2048,32,128]{3,1,2,0:T(8,128)(2,1)} %all-gather.4.cloned.1.call-done, bf16[1,256,32,128]{3,2,0,1:T(8,128)(2,1)S(1)} %copy-done.3), kind=kOutput, calls=%fused_computation.35 | convolution fusion | flops 1073741824 | bytes 23068672
  426.2 11.8 %bitcast_reduce_fusion.2 = (f32[4,64,32]{1,0,2:T(4,128)S(1)}, f32[4,64,32]{1,0,2:T(4,128)S(1)}) fusion(f32[32,512,4,64]{1,3,2,0:T(8,128)} %bitcast.145, f32[32,512,4,64]{1,3,2,0:T(8,128)} %bitcast.149), kind=kLoop, calls=%fused_computation.7 | loop fusion | flops 16760832 | bytes 33619968 | tf_op jit(solution)/shard_map/reduce_max | solution.py:13
  438.1 17.2 %fusion.4 = (f32[4,64,32]{1,0,2:T(4,128)S(1)}, bf16[4,64,32,512]{3,1,0,2:T(8,128)(2,1)}) fusion(f32[32,512,4,64]{1,3,2,0:T(8,128)} %bitcast.150, f32[4,64,32]{1,0,2:T(4,128)S(1)} %copy.48, f32[32,512,256]{1,2,0} %fusion.19), kind=kLoop, calls=%fused_computation.12 | loop fusion | flops 25157632 | bytes 42008576 | tf_op jit(solution)/shard_map/reduce_sum | solution.py:16
  456.5 6.7 %fusion.6 = (f32[4,64,32]{1,0,2:T(4,128)S(1)}, bf16[4,64,32,512]{3,1,0,2:T(8,128)(2,1)}) fusion(f32[32,512,4,64]{1,3,2,0:T(8,128)S(1)} %bitcast.146, f32[4,64,32]{1,0,2:T(4,128)S(1)} %copy.50, f32[32,512,256]{1,2,0:S(1)} %copy-done.2), kind=kLoop, calls=%fused_computation.14 | loop fusion | flops 25157632 | bytes 42008576 | tf_op jit(solution)/shard_map/reduce_sum | solution.py:16
  463.3 10.3 %fusion.16 = f32[32,512,256]{1,2,0} fusion(bf16[2,2048,32,128]{3,1,2,0:T(8,128)(2,1)} %all-gather.4.cloned.1.call-done, bf16[1,256,32,128]{3,2,0,1:T(8,128)(2,1)S(1)} %copy-done.3), kind=kOutput, calls=%fused_computation.29 | convolution fusion | flops 1073741824 | bytes 23068672
  473.6 10.3 %fusion.17 = f32[32,512,256]{1,2,0} fusion(bf16[2,2048,32,128]{3,1,2,0:T(8,128)(2,1)} %all-gather.4.cloned.1.call-done, bf16[1,256,32,128]{3,2,0,1:T(8,128)(2,1)S(1)} %copy-done.3), kind=kOutput, calls=%fused_computation.31 | convolution fusion | flops 1073741824 | bytes 23068672
  483.8 11.6 %bitcast_reduce_fusion = (f32[4,64,32]{1,0,2:T(4,128)S(1)}, f32[4,64,32]{1,0,2:T(4,128)S(1)}) fusion(f32[32,512,4,64]{1,3,2,0:T(8,128)} %bitcast.147, f32[32,512,4,64]{1,3,2,0:T(8,128)} %bitcast.143), kind=kLoop, calls=%fused_computation.1 | loop fusion | flops 16760832 | bytes 33619968 | tf_op jit(solution)/shard_map/reduce_max | solution.py:13
  496.2 4.6 all-to-all-start
  500.9 17.7 %fusion.10 = (f32[4,64,32]{1,0,2:T(4,128)S(1)}, bf16[4,64,32,512]{3,1,0,2:T(8,128)(2,1)}) fusion(f32[32,512,4,64]{1,3,2,0:T(8,128)} %bitcast.148, f32[4,64,32]{1,0,2:T(4,128)S(1)} %copy.54, f32[32,512,256]{1,2,0} %fusion.16), kind=kLoop, calls=%fused_computation.18 | loop fusion | flops 25157632 | bytes 42008576 | tf_op jit(solution)/shard_map/reduce_sum | solution.py:16
  519.4 6.8 %fusion.8 = (f32[4,64,32]{1,0,2:T(4,128)S(1)}, bf16[4,64,32,512]{3,1,0,2:T(8,128)(2,1)}) fusion(f32[32,512,4,64]{1,3,2,0:T(8,128)S(1)} %bitcast.144, f32[4,64,32]{1,0,2:T(4,128)S(1)} %copy.52, f32[32,512,256]{1,2,0:S(1)} %copy-done.1), kind=kLoop, calls=%fused_computation.16 | loop fusion | flops 25157632 | bytes 42008576 | tf_op jit(solution)/shard_map/reduce_sum | solution.py:16
  526.2 6.7 %fusion.15 = f32[32,128,256]{1,2,0} fusion(bf16[32,512,256]{1,2,0:T(8,128)(2,1)S(1)} %bitcast.153, bf16[2,2048,32,128]{3,1,2,0:T(8,128)(2,1)} %all-gather.4.cloned.1.call-done), kind=kOutput, calls=%fused_computation.27 | convolution fusion | flops 1073741824 | bytes 16777216
  532.9 9.0 %fusion.14 = f32[32,128,256]{1,2,0} fusion(bf16[32,512,256]{1,2,0:T(8,128)(2,1)} %bitcast.154, bf16[2,2048,32,128]{3,1,2,0:T(8,128)(2,1)} %all-gather.4.cloned.1.call-done), kind=kOutput, calls=%fused_computation.25 | convolution fusion | flops 1073741824 | bytes 16777216
  541.9 6.6 %fusion.12 = f32[32,128,256]{1,2,0} fusion(bf16[32,512,256]{1,2,0:T(8,128)(2,1)S(1)} %bitcast.157, bf16[2,2048,32,128]{3,1,2,0:T(8,128)(2,1)} %all-gather.4.cloned.1.call-done), kind=kOutput, calls=%fused_computation.21 | convolution fusion | flops 1073741824 | bytes 16777216
  548.5 6.6 %fusion.13 = f32[32,128,256]{1,2,0} fusion(bf16[32,512,256]{1,2,0:T(8,128)(2,1)S(1)} %bitcast.160, bf16[2,2048,32,128]{3,1,2,0:T(8,128)(2,1)} %all-gather.4.cloned.1.call-done), kind=kOutput, calls=%fused_computation.23 | convolution fusion | flops 1073741824 | bytes 16777216
  556.1 4.8 all-to-all-start.2
  560.9 7.4 %multiply_add_fusion = f32[4,64,32,128]{3,1,0,2:T(8,128)S(1)} fusion(f32[4,64,32,128]{3,1,0,2:T(8,128)} %bitcast.163, f32[4,64,32,128]{3,1,0,2:T(8,128)} %bitcast.164, f32[4,64,32,128]{3,1,0,2:T(8,128)} %bitcast.162, f32[4,64,32,128]{3,1,0,2:T(8,128)} %bitcast.161, f32[4,64,32]{1,0,2:T(4,128)S(1)} %copy.53, f32[4,64,32]{1,0,2:T(4,128)S(1)} %copy.51, ...), kind=kLoop, calls=%fused_computation.37 | loop fusion | flops 7340032 | bytes 21102592 | tf_op jit(solution)/shard_map/add | solution.py:17
  568.3 2.2 copy.55
  570.6 4.9 all-to-all-start.1
  579.9 44.4 %all-to-all-done.1 = f32[4,64,32,128]{3,1,2,0:T(8,128)} async-done(((f32[4,64,32,128]{3,1,2,0:T(8,128)}), f32[4,64,32,128]{3,1,2,0:T(8,128)}, u32[]{:S(2)}, u32[]{:S(2)}) %all-to-all-start.1) | async-done | bytes 4194336 | tf_op jit(solution)/shard_map/all_to_all | solution.py:46
  624.3 2.9 multiply_reduce_fusion
  (64 shorter events, 12.9 us)
Async XLA Ops:
  6.5 570.0 %copy-start = (f32[8,32,128]{2,1,0:T(8,128)S(1)}, f32[8,32,128]{2,1,0:T(8,128)}, u32[]{:S(2)}) copy-start(f32[8,32,128]{2,1,0:T(8,128)} %param.10) | copy-start | bytes 393220
  6.5 32.7 %all-gather.6.cloned.1.call-start = ((), (), s32[]{:S(2)}) async-start(), calls=%async_computation.4 | async-start | bytes 2621440 | tf_op jit(solution)/shard_map/all_gather | solution.py:73
  7.3 397.7 %all-gather.4.cloned.1.call-start = ((), (), s32[]{:S(2)}) async-start(), calls=%async_computation.3 | async-start | bytes 34603008 | tf_op jit(solution)/shard_map/all_gather | solution.py:82
  39.3 376.6 %copy-start.3 = (bf16[1,256,32,128]{3,2,0,1:T(8,128)(2,1)S(1)}, bf16[1,256,32,128]{3,2,0,1:T(8,128)(2,1)}, u32[]{:S(2)}) copy-start(bf16[1,256,32,128]{3,2,0,1:T(8,128)(2,1)} %all-gather.6.cloned.1.call-done) | copy-start | bytes 6291460
  438.1 18.5 %copy-start.2 = (f32[32,512,256]{1,2,0:S(1)}, f32[32,512,256]{1,2,0}, u32[]{:S(2)}) copy-start(f32[32,512,256]{1,2,0} %fusion.18) | copy-start | bytes 50331652
  496.2 59.8 %all-to-all-start = ((f32[4,1,2048]{2,1,0:T(1,128)}), f32[4,1,2048]{2,1,0:T(1,128)S(1)}, u32[]{:S(2)}, u32[]{:S(2)}) async-start(f32[4,1,2048]{2,1,0:T(1,128)} %reshape.99), calls=%async_computation | async-start | bytes 65536 | tf_op jit(solution)/shard_map/all_to_all | solution.py:44
  500.9 18.5 %copy-start.1 = (f32[32,512,256]{1,2,0:S(1)}, f32[32,512,256]{1,2,0}, u32[]{:S(2)}) copy-start(f32[32,512,256]{1,2,0} %fusion.17) | copy-start | bytes 50331652
  500.9 25.2 %slice-start = ((s8[8388608]{0:T(1024)(128)(4,1)}), s8[4194304]{0:T(1024)(128)(4,1)S(1)}, s32[]{:S(2)}) async-start(s8[8388608]{0:T(1024)(128)(4,1)} %bitcast.151), calls=%async_computation.5 | async-start | bytes 8388608
  518.5 7.6 %slice-start.1 = ((s8[8388608]{0:T(1024)(128)(4,1)}), s8[4194304]{0:T(1024)(128)(4,1)S(1)}, s32[]{:S(2)}) async-start(s8[8388608]{0:T(1024)(128)(4,1)} %bitcast.151), calls=%async_computation.6 | async-start | bytes 8388608
  526.1 15.8 %slice-start.2 = ((s8[8388608]{0:T(1024)(128)(4,1)}), s8[4194304]{0:T(1024)(128)(4,1)S(1)}, s32[]{:S(2)}) async-start(s8[8388608]{0:T(1024)(128)(4,1)} %bitcast.155), calls=%async_computation.7 | async-start | bytes 8388608
  532.9 9.0 %slice-start.3 = ((s8[8388608]{0:T(1024)(128)(4,1)}), s8[4194304]{0:T(1024)(128)(4,1)S(1)}, s32[]{:S(2)}) async-start(s8[8388608]{0:T(1024)(128)(4,1)} %bitcast.155), calls=%async_computation.8 | async-start | bytes 8388608
  532.9 15.6 %slice-start.4 = ((s8[8388608]{0:T(1024)(128)(4,1)}), s8[4194304]{0:T(1024)(128)(4,1)S(1)}, s32[]{:S(2)}) async-start(s8[8388608]{0:T(1024)(128)(4,1)} %bitcast.158), calls=%async_computation.9 | async-start | bytes 8388608
  541.9 6.6 %slice-start.5 = ((s8[8388608]{0:T(1024)(128)(4,1)}), s8[4194304]{0:T(1024)(128)(4,1)S(1)}, s32[]{:S(2)}) async-start(s8[8388608]{0:T(1024)(128)(4,1)} %bitcast.158), calls=%async_computation.10 | async-start | bytes 8388608
  556.1 14.5 %all-to-all-start.2 = ((f32[4,1,2048]{2,1,0:T(1,128)}), f32[4,1,2048]{2,1,0:T(1,128)S(1)}, u32[]{:S(2)}, u32[]{:S(2)}) async-start(f32[4,1,2048]{2,1,0:T(1,128)} %reshape.101), calls=%async_computation.2 | async-start | bytes 65536 | tf_op jit(solution)/shard_map/all_to_all | solution.py:45
  568.3 7.2 %copy-start.5 = (s32[4]{0:T(128)S(1)}, s32[4]{0:T(128)}, u32[]{:S(2)}) copy-start(s32[4]{0:T(128)} %param.11) | copy-start | bytes 52
  568.3 7.8 %copy-start.4 = (s32[4,4]{1,0:T(4,128)S(1)}, s32[4,4]{1,0:T(4,128)}, u32[]{:S(2)}) copy-start(s32[4,4]{1,0:T(4,128)} %param.13) | copy-start | bytes 196
  568.3 7.8 %copy-start.6 = (s32[4]{0:T(128)S(1)}, s32[4]{0:T(128)}, u32[]{:S(2)}) copy-start(s32[4]{0:T(128)} %param.12) | copy-start | bytes 52
  570.6 53.7 %all-to-all-start.1 = ((f32[4,64,32,128]{3,1,2,0:T(8,128)}), f32[4,64,32,128]{3,1,2,0:T(8,128)}, u32[]{:S(2)}, u32[]{:S(2)}) async-start(f32[4,64,32,128]{3,1,2,0:T(8,128)} %copy.55), calls=%async_computation.1 | async-start | bytes 8388608 | tf_op jit(solution)/shard_map/all_to_all | solution.py:46
Sparse Core Ops, SparseCore 0:
  9.0 30.2 all-gather.5
  40.9 363.9 all-gather.3
where the time goes:
time: 636 us
  waiting for transfers between devices  439 us (69%)
  other arithmetic  85.8 us (13%)
  matrix products  72.2 us (11%)
  starting transfers between devices  14.4 us (2%)
  between operations  13.7 us (2%)
  local copies, waits for them, and re-layouts  10.4 us (2%)
    all_gather x1, waiting for transfers between devices, shards(): shard_rows = lax.all_gather(paired, 'ctx', axis=1, tiled=True)  366 us
    unnamed x8, matrix products  70.7 us
    reduce_sum x4, other arithmetic, flash_update(): total = total * rescale + jnp.sum(weights, axis=-1)  48.4 us
    all_to_all x1, waiting for transfers between devices, finish_tokens(): lax.all_to_all(mixed, 'queue', split_axis=0, concat_axis=0, tiled=True)  44.4 us
    all_gather x1, waiting for transfers between devices, shards(): gathered = lax.all_gather(query_local, 'queue', axis=0, tiled=True)  28.4 us
    reduce_max x2, other arithmetic, flash_update(): new_max = jnp.maximum(row_max, jnp.max(scores, axis=-1))  23.4 us
  transfers between devices with their start and end apart: 5, of which 3 were waited for; matrix products, arithmetic and copies ran while one was open for 11% of the time, Pallas kernels for 0%

commit v1 on v0

v1 whole, which is shorter than its diff:
```python
import functools

import jax
import jax.numpy as jnp
from jax import lax
from jax.experimental import pallas as pl
from jax.experimental.pallas import tpu as pltpu
from jax.sharding import Mesh, PartitionSpec as P

LOG2E = 1.4426950408889634
SWAP = [(0, 1), (1, 0)]


def attend_kernel(
    place, order, levels, mask, own, other, gates, out, q_all, row_max, total, mixed, *, toks, share
):
    core, head = place[0], place[1]
    groups = own.shape[0] // 2
    size = own.shape[-1]
    rows = groups * share
    keys = groups * toks
    scale = LOG2E / size**0.5
    row_max[...] = jnp.full(row_max.shape, -1e30, jnp.float32)
    total[...] = jnp.zeros(total.shape, jnp.float32)
    mixed[...] = jnp.zeros(mixed.shape, jnp.float32)
    start = pl.multiple_of(2 * toks + core * share, 16)

    def stretch_of(slot):
        return 2 * (slot % 2) + jnp.where(slot < 2, core, 1 - core)

    for slot in range(4):
        src = own if slot < 2 else other
        part = src[pl.ds((slot % 2) * groups, groups), pl.ds(start, share), :]
        q_all[slot] = part.reshape(rows, size)

    for key_slot in range(4):
        src = own if key_slot < 2 else other
        key_pos = order[stretch_of(key_slot)]
        lo = (key_slot % 2) * groups

        @pl.loop(0, 4)
        def _(query_slot, src=src, lo=lo, key_pos=key_pos):
            query_pos = order[stretch_of(query_slot)]

            @pl.when(mask[query_pos, key_pos] == 1)
            def _():
                k = src[lo : lo + groups, 0:toks, :].reshape(keys, size)
                v = src[lo : lo + groups, toks : 2 * toks, :].reshape(keys, size)
                sub = 128
                for r in range(0, rows, sub):
                    at = (query_slot, slice(r, r + sub), slice(None))
                    q = q_all[at]
                    s = lax.dot_general(
                        q, k, (((1,), (1,)), ((), ())), preferred_element_type=jnp.float32
                    )
                    old = row_max[at][:, 0:1]
                    new = jnp.maximum(old, jnp.max(s, axis=1, keepdims=True))
                    keep = jnp.exp2((old - new) * scale)
                    p = jnp.exp2((s - new) * scale)
                    row_max[at] = jnp.broadcast_to(new, (sub, size))
                    total[at] = total[at] * keep + jnp.sum(p, axis=1, keepdims=True)
                    mixed[at] = mixed[at] * keep + jnp.dot(
                        p.astype(jnp.bfloat16), v, preferred_element_type=jnp.float32
                    )

    for slot in range(4):
        stretch = stretch_of(slot)
        gate = gates[levels[stretch], pl.ds(head, 1), :]
        result = mixed[slot] / total[slot] * gate
        out[stretch] = result.astype(jnp.bfloat16).reshape(groups, share, size)


def attend(place, order, levels, mask, own, other, gates, toks, share):
    groups, size = own.shape[0] // 2, own.shape[-1]
    rows = groups * share
    smem = pl.BlockSpec(memory_space=pltpu.SMEM)
    vmem = pl.BlockSpec(memory_space=pltpu.VMEM)
    return pl.pallas_call(
        functools.partial(attend_kernel, toks=toks, share=share),
        out_shape=jax.ShapeDtypeStruct((4, groups, share, size), jnp.bfloat16),
        in_specs=[smem, smem, smem, smem, vmem, vmem, vmem],
        out_specs=vmem,
        scratch_shapes=[
            pltpu.VMEM((4, rows, size), jnp.bfloat16),
            pltpu.VMEM((4, rows, size), jnp.float32),
            pltpu.VMEM((4, rows, size), jnp.float32),
            pltpu.VMEM((4, rows, size), jnp.float32),
        ],
        compiler_params=pltpu.CompilerParams(vmem_limit_bytes=48 * 2**20),
    )(place, order, levels, mask, own, other, gates)


def shards(queries, keys, values, gate_table, noise_level, stretch_order, block_mask):
    toks, heads, size = queries.shape[1:]
    half, share = toks // 2, toks // 4
    k = jnp.swapaxes(keys[0], 0, 1)
    v = jnp.swapaxes(values[0], 0, 1)
    q = jnp.swapaxes(queries[0].reshape(2, half, heads, size), 1, 2)
    kv = jnp.concatenate([k, v], axis=1)
    send = jnp.concatenate([jnp.broadcast_to(kv[None], (2,) + kv.shape), q], axis=2)
    send = send.reshape(2 * heads, 2 * toks + half, size)
    own = lax.all_to_all(send, ("xh", "ctx"), 0, 0, tiled=True)
    other = lax.ppermute(own, "core", SWAP)
    place = jnp.stack([lax.axis_index("core"), lax.axis_index("ctx")]).astype(jnp.int32)
    part = attend(place, stretch_order, noise_level, block_mask, own, other, gate_table, toks, share)
    back = lax.all_to_all(
        part.reshape(4 * heads, share, size), ("xh", "core", "ctx"), 0, 0, tiled=True
    )
    back = back.reshape(4, heads, share, size)
    return jnp.swapaxes(back, 1, 2).reshape(1, toks, heads, size)


def solution(mesh):
    wide = Mesh(mesh.devices.reshape(2, 2, -1), ("xh", "core", "ctx"))
    tokens = P(("xh", "core"), "ctx", None, None)
    return jax.shard_map(
        shards,
        mesh=wide,
        in_specs=(tokens, tokens, tokens, P(), P(), P(), P()),
        out_specs=tokens,
        check_vma=False,
    )
```

time: 636 us -> 95.8 us (0.15)
  waiting for transfers between devices: 439 us -> 4.59 us
  other arithmetic: 85.8 us -> 1.57 us
  matrix products: 72.2 us -> 0 us
  blocking collectives: 0 us -> 63.3 us
  Pallas kernels: 0 us -> 19.2 us
  between operations: 13.7 us -> 0.08 us
  starting transfers between devices: 14.4 us -> 2.46 us
  local copies, waits for them, and re-layouts: 10.4 us -> 3.1 us
    all_gather x2 -> x0, waiting for transfers between devices: 394 us -> none  [the longest x1 366 us: shards(): shard_rows = lax.all_gather(paired, 'ctx', axis=1, tiled=True)]
    unnamed x8 -> x0, matrix products: 70.7 us -> none
    all_to_all x0 -> x2, blocking collectives: none -> 63.3 us  [the longest x1 46 us: shards(): own = lax.all_to_all(send, ('xh', 'ctx'), 0, 0, tiled=True)]
    reduce_sum x7 -> x0, other arithmetic: 52 us -> none  [the longest x4 48.4 us: flash_update(): total = total * rescale + jnp.sum(weights, axis=-1)]
    all_to_all x3 -> x0, waiting for transfers between devices: 44.4 us -> none  [the longest x1 44.4 us: finish_tokens(): lax.all_to_all(mixed, 'queue', split_axis=0, concat_axis=0, tiled=True)]
    reduce_max x3 -> x0, other arithmetic: 23.5 us -> none  [the longest x2 23.4 us: flash_update(): new_max = jnp.maximum(row_max, jnp.max(scores, axis=-1))]
    pallas_call x0 -> x1, Pallas kernels: none -> 19.2 us  [attend(): pl.pallas_call(functools.partial(attend_kernel, toks=toks, share=share),...]
    all_to_all x3 -> x0, starting transfers between devices: 14.3 us -> none  [the longest x1 4.87 us: finish_tokens(): lax.all_to_all(mixed, 'queue', split_axis=0, concat_axis=0, tiled=True)]
  transfers between devices with their start and end apart: 5 -> 1, of which waited for: 3 -> 1; matrix products, arithmetic and copies ran while one was open for 11% -> 0% of each run, Pallas kernels for 0% -> 0%
where the time goes in v1:
time: 95.8 us; the launch traced here: 94.3 us
  blocking collectives  63.3 us (66%)
  Pallas kernels  19.2 us (20%)
  waiting for transfers between devices  4.59 us (5%)
  local copies, waits for them, and re-layouts  3.1 us (3%)
  starting transfers between devices  2.46 us (3%)
  other arithmetic  1.57 us (2%)
    all_to_all x1, blocking collectives, shards(): own = lax.all_to_all(send, ('xh', 'ctx'), 0, 0, tiled=True)  46 us
    pallas_call x1, Pallas kernels, attend(): pl.pallas_call(functools.partial(attend_kernel, toks=toks, share=share),...  19.2 us
    all_to_all x1, blocking collectives, shards(): lax.all_to_all(part.reshape(4 * heads, share, size), ('xh', 'core', 'ctx'...  17.3 us
    ppermute x1, waiting for transfers between devices, shards(): other = lax.ppermute(own, 'core', SWAP)  4.59 us
    ppermute x1, starting transfers between devices, shards(): other = lax.ppermute(own, 'core', SWAP)  2.46 us
  transfers between devices with their start and end apart: 1, of which 1 were waited for; matrix products, arithmetic and copies ran while one was open for 0% of the time, Pallas kernels for 0%

profile of v1, /device:TPU:1, one launch (start us, length us, event | category | flops | bytes accessed | tf_op | source)
XLA Modules:
  0.0 94.3 jit_solution(11667961684211457789)
XLA Ops:
  0.0 1.2 %copy.12 = bf16[2,32,32,128]{3,1,2,0:T(8,128)(2,1)S(1)} copy(bf16[2,32,32,128]{3,2,1,0:T(8,128)(2,1)} %bitcast.22) | data formatting | bytes 1048576 | tf_op jit(solution)/shard_map/reshape;squeeze | solution.py:98
  1.2 1.3 %pad_maximum_fusion.1 = bf16[32,128,128]{2,0,1:T(8,128)(2,1)S(1)} fusion(bf16[32,64,128]{2,0,1:T(8,128)(2,1)} %bitcast.23, bf16[32,64,128]{2,0,1:T(8,128)(2,1)} %bitcast.24), kind=kLoop, calls=%fused_computation.1 | loop fusion | flops 524288 | bytes 2097152 | tf_op jit(solution)/shard_map/concatenate | solution.py:99
  2.5 0.4 copy.8
  3.0 0.5 broadcast_in_dim.2
  3.5 0.2 pad_maximum_fusion
  3.7 0.0 copy-start
  3.7 0.0 copy-start.1
  3.7 0.0 copy-start.2
  3.7 0.0 copy-start.3
  3.7 46.0 %all_to_all.10.own = bf16[64,160,128]{2,1,0:T(8,128)(2,1)S(1)} all-to-all(bf16[64,160,128]{2,1,0:T(8,128)(2,1)S(1)} %bitcast.19), channel_id=1, replica_groups=mesh['xh'=2,'core'=2,'ctx'=32] {'xh','ctx'}, dimensions={0} | all-to-all | bytes 5242880 | tf_op jit(solution)/shard_map/all_to_all | solution.py:102
  49.7 2.5 %collective-permute-start = (bf16[64,160,128]{2,1,0:T(8,128)(2,1)S(1)}, bf16[64,160,128]{2,1,0:T(8,128)(2,1)}, u32[]{:S(2)}, u32[]{:S(2)}) collective-permute-start(bf16[64,160,128]{2,1,0:T(8,128)(2,1)S(1)} %all_to_all.10.own), channel_id=1, source_target_pairs={{0,32},{32,0},{1,33},{33,1},{2,34},{34,2},{3,35},{35,3},{4,36},{36... | collective-permute-start | bytes 7864328 | tf_op jit(solution)/shard_map/ppermute | solution.py:103
  52.1 0.1 pad_add_fusion.place
  52.2 4.6 %collective-permute-done.other = bf16[64,160,128]{2,1,0:T(8,128)(2,1)} collective-permute-done((bf16[64,160,128]{2,1,0:T(8,128)(2,1)S(1)}, bf16[64,160,128]{2,1,0:T(8,128)(2,1)}, u32[]{:S(2)}, u32[]{:S(2)}) %collective-permute-start) | collective-permute-done | bytes 2621472 | tf_op jit(solution)/shard_map/ppermute | solution.py:103
  56.8 0.0 copy-done
  56.8 0.0 copy-done.1
  56.8 0.0 copy-done.2
  56.8 0.0 copy-done.3
  56.8 19.2 %shard_map.73 = bf16[4,32,16,128]{3,2,1,0:T(8,128)(2,1)S(1)} custom-call(s32[2]{0:T(128)S(1)} %pad_add_fusion.place, s32[4]{0:T(128)S(1)} %copy-done.2, s32[4]{0:T(128)S(1)} %copy-done.3, s32[4,4]{1,0:T(4,128)S(1)} %copy-done.1, bf16[64,160,128]{2,1,0:T(8,128)(2,1)S(1)} %all_to_all.10.own, bf16[64,160,128]{2,1,0:T(8,128)(2,1)} %collective-permute-done.other, ...), custom_call_target="tpu_custom_call" | custom-call | tf_op jit(solution)/shard_map/pallas_call | solution.py:78
  76.0 17.3 %all_to_all.11 = bf16[128,16,128]{2,1,0:T(8,128)(2,1)S(1)} all-to-all(bf16[128,16,128]{2,1,0:T(8,128)(2,1)S(1)} %bitcast.18), channel_id=1, replica_groups=mesh['xh'=2,'core'=2,'ctx'=32] {'xh','core','ctx'}, dimensions={0} | all-to-all | bytes 1048576 | tf_op jit(solution)/shard_map/all_to_all | solution.py:106
  93.4 0.9 copy.10
Async XLA Ops:
  3.7 53.1 %copy-start = (f32[8,32,128]{2,1,0:T(8,128)S(1)}, f32[8,32,128]{2,1,0:T(8,128)}, u32[]{:S(2)}) copy-start(f32[8,32,128]{2,1,0:T(8,128)} %gates.1) | copy-start | bytes 393220
  3.7 53.1 %copy-start.1 = (s32[4,4]{1,0:T(4,128)S(1)}, s32[4,4]{1,0:T(4,128)}, u32[]{:S(2)}) copy-start(s32[4,4]{1,0:T(4,128)} %mask.1) | copy-start | bytes 196
  3.7 53.1 %copy-start.2 = (s32[4]{0:T(128)S(1)}, s32[4]{0:T(128)}, u32[]{:S(2)}) copy-start(s32[4]{0:T(128)} %order.1) | copy-start | bytes 52
  3.7 53.1 %copy-start.3 = (s32[4]{0:T(128)S(1)}, s32[4]{0:T(128)}, u32[]{:S(2)}) copy-start(s32[4]{0:T(128)} %levels.1) | copy-start | bytes 52
  49.7 7.1 %collective-permute-start = (bf16[64,160,128]{2,1,0:T(8,128)(2,1)S(1)}, bf16[64,160,128]{2,1,0:T(8,128)(2,1)}, u32[]{:S(2)}, u32[]{:S(2)}) collective-permute-start(bf16[64,160,128]{2,1,0:T(8,128)(2,1)S(1)} %all_to_all.10.own), channel_id=1, source_target_pairs={{0,32},{32,0},{1,33},{33,1},{2,34},{34,2},{3,35},{35,3},{4,36},{36... | collective-permute-start | bytes 7864328 | tf_op jit(solution)/shard_map/ppermute | solution.py:103

commit v2 on v1

v2 whole, which is shorter than its diff:
```python
import functools

import jax
import jax.numpy as jnp
from jax import lax
from jax.experimental import pallas as pl
from jax.experimental.pallas import tpu as pltpu
from jax.sharding import Mesh, PartitionSpec as P

LOG2E = 1.4426950408889634
SWAP = [(0, 1), (1, 0)]


BOTH = (((1,), (1,)), ((), ()))
def attend_kernel(place, order, levels, mask, own, other, gates, out,
           pair_q, pair_k, q_all, k_all, v_all, run_max, total, mixed, s_a, s_b, m_a, m_b, f_a, f_b, *, toks, share, kd, kt):
    core, head = place[0], place[1]
    groups = own.shape[0] // 2
    size = own.shape[-1]
    rows = groups * share
    keys = groups * toks
    scale = LOG2E / size**0.5
    run_max[...] = jnp.full(run_max.shape, -1e30, jnp.float32)
    total[...] = jnp.zeros(total.shape, jnp.float32)
    mixed[...] = jnp.zeros(mixed.shape, jnp.float32)
    start = pl.multiple_of(2 * toks + core * share, 16)
    spot = lax.broadcasted_iota(jnp.int32, (size, size), 0) == lax.broadcasted_iota(jnp.int32, (size, size), 1)
    eye = jnp.where(spot, 1.0, 0.0).astype(jnp.bfloat16)

    def stretch_of(slot):
        return 2 * (slot % 2) + jnp.where(slot < 2, core, 1 - core)

    for slot in range(4):
        src = own if slot < 2 else other
        at = pl.ds((slot % 2) * groups, groups)
        q = src[at, pl.ds(start, share), :].reshape(rows, size).astype(jnp.float32) * scale
        high = q.astype(jnp.bfloat16)
        q_all[slot, :, 0:size] = high
        q_all[slot, :, size:] = (q - high.astype(jnp.float32)).astype(jnp.bfloat16)
        k_all[slot] = src[at, 0:toks, :].reshape(keys, size)
        v = src[at, toks : 2 * toks, :].reshape(keys, size)
        v_all[slot] = lax.dot_general(eye, v, BOTH, preferred_element_type=jnp.float32).astype(jnp.bfloat16)

    count = jnp.int32(0)
    for key_slot in range(4):
        for query_slot in range(4):
            pair_q[count] = query_slot
            pair_k[count] = key_slot
            hit = mask[order[stretch_of(query_slot)], order[stretch_of(key_slot)]] == 1
            count = count + hit.astype(jnp.int32)

    def step(n, s_new, m_new, f_new, s_old, m_old, f_old, fresh=True, used=True):
        if fresh:
            nn = jnp.minimum(n + 1, count - 1)
            qn, kn = pair_q[nn], pair_k[nn]
            q = q_all[qn]
            best = None
        if used:
            qs, ks = pair_q[n], pair_k[n]
            m = m_old[0:1, :]
            f = f_old[0:1, :]
            parts, tots, acc = [], None, None
        for c in range(0, keys, kt):
            if fresh:
                k = k_all[kn, c : c + kt, :]
                s = lax.dot_general(jnp.concatenate([k, k], axis=1), q, BOTH, preferred_element_type=jnp.float32)
                s_new[c : c + kt, :] = s
                top = jnp.max(s.reshape(kt // 8, 8, rows), axis=0)
                best = top if best is None else jnp.maximum(best, top)
            if used:
                p = jnp.exp2(s_old[c : c + kt, :] - m)
                t = jnp.sum(p.reshape(kt // 8, 8, rows), axis=0)
                tots = t if tots is None else tots + t
                parts.append(p.astype(jnp.bfloat16))
                if len(parts) * kt == kd:
                    d = jnp.dot(v_all[ks, :, c + kt - kd : c + kt], jnp.concatenate(parts, axis=0), preferred_element_type=jnp.float32)
                    acc = d if acc is None else acc + d
                    parts = []
        if used:
            total[qs] = total[qs] * f + tots
            mixed[qs] = mixed[qs] * f + acc
        if fresh:
            old = run_max[qn]
            new = jnp.maximum(old, jnp.max(best, axis=0, keepdims=True))
            run_max[qn] = new
            m_new[...] = new
            f_new[...] = jnp.exp2(old - new)

    a, b = (s_a, m_a, f_a), (s_b, m_b, f_b)
    step(-1, *a, *b, used=False)

    @pl.loop(0, (count + 1) // 2)
    def _(t):
        step(2 * t, *b, *a)

        @pl.when(2 * t + 1 < count)
        def _():
            step(2 * t + 1, *a, *b)

    for slot in range(4):
        stretch = stretch_of(slot)
        gate = gates[levels[stretch], pl.ds(head, 1), :]
        o = mixed[slot] / jnp.sum(total[slot], axis=0, keepdims=True)
        out[stretch] = (o.T * gate).astype(jnp.bfloat16).reshape(groups, share, size)

def attend(place, order, levels, mask, own, other, gates, toks, share, kd=512, kt=512):
    groups, size = own.shape[0] // 2, own.shape[-1]
    rows, keys = groups * share, groups*toks
    smem = pl.BlockSpec(memory_space=pltpu.SMEM)
    vmem = pl.BlockSpec(memory_space=pltpu.VMEM)
    f32, bf16 = jnp.float32, jnp.bfloat16
    return pl.pallas_call(
        functools.partial(attend_kernel, toks=toks, share=share, kd=kd, kt=kt),
        out_shape=jax.ShapeDtypeStruct((4, groups, share, size), jnp.bfloat16),
        in_specs=[smem, smem, smem, smem, vmem, vmem, vmem],
        out_specs=vmem,
        scratch_shapes=[
            pltpu.SMEM((17,), jnp.int32), pltpu.SMEM((17,), jnp.int32),
            pltpu.VMEM((4, rows, 2*size), bf16),
            pltpu.VMEM((4, keys, size), bf16),
            pltpu.VMEM((4, size, keys), bf16),
            pltpu.VMEM((4, 8, rows), f32),
            pltpu.VMEM((4, 8, rows), f32),
            pltpu.VMEM((4, size, rows), f32),
            pltpu.VMEM((keys, rows), f32), pltpu.VMEM((keys, rows), f32),
            pltpu.VMEM((8, rows), f32), pltpu.VMEM((8, rows), f32),
            pltpu.VMEM((8, rows), f32), pltpu.VMEM((8, rows), f32),
        ],
        compiler_params=pltpu.CompilerParams(vmem_limit_bytes=48 * 2**20),
    )(place, order, levels, mask, own, other, gates)


def shards(queries, keys, values, gate_table, noise_level, stretch_order, block_mask):
    toks, heads, size = queries.shape[1:]
    half, share = toks // 2, toks // 4
    k = jnp.swapaxes(keys[0], 0, 1)
    v = jnp.swapaxes(values[0], 0, 1)
    q = jnp.swapaxes(queries[0].reshape(2, half, heads, size), 1, 2)
    kv = jnp.concatenate([k, v], axis=1)
    send = jnp.concatenate([jnp.broadcast_to(kv[None], (2,) + kv.shape), q], axis=2)
    send = send.reshape(2 * heads, 2 * toks + half, size)
    own = lax.all_to_all(send, ("xh", "ctx"), 0, 0, tiled=True)
    other = lax.ppermute(own, "core", SWAP)
    place = jnp.stack([lax.axis_index("core"), lax.axis_index("ctx")]).astype(jnp.int32)
    part = attend(place, stretch_order, noise_level, block_mask, own, other, gate_table, toks, share)
    back = lax.all_to_all(
        part.reshape(4 * heads, share, size), ("xh", "core", "ctx"), 0, 0, tiled=True
    )
    back = back.reshape(4, heads, share, size)
    return jnp.swapaxes(back, 1, 2).reshape(1, toks, heads, size)


def solution(mesh):
    wide = Mesh(mesh.devices.reshape(2, 2, -1), ("xh", "core", "ctx"))
    tokens = P(("xh", "core"), "ctx", None, None)
    return jax.shard_map(
        shards,
        mesh=wide,
        in_specs=(tokens, tokens, tokens, P(), P(), P(), P()),
        out_specs=tokens,
        check_vma=False,
    )
```

time: 95.8 us -> 91 us (0.950)
  Pallas kernels: 19.2 us -> 15 us
    pallas_call x1, Pallas kernels: 19.2 us -> 15 us  [attend(): pl.pallas_call(functools.partial(attend_kernel, toks=toks, share=share, k...]
where the time goes in v2:
time: 91 us; the launch traced here: 90.1 us
  blocking collectives  63.3 us (70%)
  Pallas kernels  15 us (16%)
  waiting for transfers between devices  4.59 us (5%)
  local copies, waits for them, and re-layouts  3.1 us (3%)
  starting transfers between devices  2.46 us (3%)
  other arithmetic  1.57 us (2%)
    all_to_all x1, blocking collectives, shards(): own = lax.all_to_all(send, ('xh', 'ctx'), 0, 0, tiled=True)  46 us
    all_to_all x1, blocking collectives, shards(): lax.all_to_all(part.reshape(4 * heads, share, size), ('xh', 'core', 'ctx'...  17.3 us
    pallas_call x1, Pallas kernels, attend(): pl.pallas_call(functools.partial(attend_kernel, toks=toks, share=share, k...  15 us
    ppermute x1, waiting for transfers between devices, shards(): other = lax.ppermute(own, 'core', SWAP)  4.59 us
    ppermute x1, starting transfers between devices, shards(): other = lax.ppermute(own, 'core', SWAP)  2.46 us
  transfers between devices with their start and end apart: 1, of which 1 were waited for; matrix products, arithmetic and copies ran while one was open for 0% of the time, Pallas kernels for 0%

profile of v2, /device:TPU:1, one launch (start us, length us, event | category | flops | bytes accessed | tf_op | source)
XLA Modules:
  0.0 90.1 jit_solution(16075767428219702485)
XLA Ops:
  0.0 1.2 %copy.12 = bf16[2,32,32,128]{3,1,2,0:T(8,128)(2,1)S(1)} copy(bf16[2,32,32,128]{3,2,1,0:T(8,128)(2,1)} %bitcast.22) | data formatting | bytes 1048576 | tf_op jit(solution)/shard_map/reshape;squeeze | solution.py:138
  1.2 1.3 %pad_maximum_fusion.1 = bf16[32,128,128]{2,0,1:T(8,128)(2,1)S(1)} fusion(bf16[32,64,128]{2,0,1:T(8,128)(2,1)} %bitcast.23, bf16[32,64,128]{2,0,1:T(8,128)(2,1)} %bitcast.24), kind=kLoop, calls=%fused_computation.1 | loop fusion | flops 524288 | bytes 2097152 | tf_op jit(solution)/shard_map/concatenate | solution.py:139
  2.5 0.4 copy.8
  3.0 0.5 broadcast_in_dim.2
  3.5 0.2 pad_maximum_fusion
  3.7 0.0 copy-start
  3.7 0.0 copy-start.1
  3.7 0.0 copy-start.2
  3.7 0.0 copy-start.3
  3.7 46.0 %all_to_all.10.own = bf16[64,160,128]{2,1,0:T(8,128)(2,1)S(1)} all-to-all(bf16[64,160,128]{2,1,0:T(8,128)(2,1)S(1)} %bitcast.19), channel_id=1, replica_groups=mesh['xh'=2,'core'=2,'ctx'=32] {'xh','ctx'}, dimensions={0} | all-to-all | bytes 5242880 | tf_op jit(solution)/shard_map/all_to_all | solution.py:142
  49.7 2.5 %collective-permute-start = (bf16[64,160,128]{2,1,0:T(8,128)(2,1)S(1)}, bf16[64,160,128]{2,1,0:T(8,128)(2,1)}, u32[]{:S(2)}, u32[]{:S(2)}) collective-permute-start(bf16[64,160,128]{2,1,0:T(8,128)(2,1)S(1)} %all_to_all.10.own), channel_id=1, source_target_pairs={{0,32},{32,0},{1,33},{33,1},{2,34},{34,2},{3,35},{35,3},{4,36},{36... | collective-permute-start | bytes 7864328 | tf_op jit(solution)/shard_map/ppermute | solution.py:143
  52.1 0.1 pad_add_fusion.place
  52.2 4.6 %collective-permute-done.other = bf16[64,160,128]{2,1,0:T(8,128)(2,1)} collective-permute-done((bf16[64,160,128]{2,1,0:T(8,128)(2,1)S(1)}, bf16[64,160,128]{2,1,0:T(8,128)(2,1)}, u32[]{:S(2)}, u32[]{:S(2)}) %collective-permute-start) | collective-permute-done | bytes 2621472 | tf_op jit(solution)/shard_map/ppermute | solution.py:143
  56.8 0.0 copy-done
  56.8 0.0 copy-done.1
  56.8 0.0 copy-done.2
  56.8 0.0 copy-done.3
  56.8 15.0 %shard_map.73 = bf16[4,32,16,128]{3,2,1,0:T(8,128)(2,1)S(1)} custom-call(s32[2]{0:T(128)S(1)} %pad_add_fusion.place, s32[4]{0:T(128)S(1)} %copy-done.2, s32[4]{0:T(128)S(1)} %copy-done.3, s32[4,4]{1,0:T(4,128)S(1)} %copy-done.1, bf16[64,160,128]{2,1,0:T(8,128)(2,1)S(1)} %all_to_all.10.own, bf16[64,160,128]{2,1,0:T(8,128)(2,1)} %collective-permute-done.other, ...), custom_call_target="tpu_custom_call" | custom-call | tf_op jit(solution)/shard_map/pallas_call | solution.py:112
  71.8 17.3 %all_to_all.11 = bf16[128,16,128]{2,1,0:T(8,128)(2,1)S(1)} all-to-all(bf16[128,16,128]{2,1,0:T(8,128)(2,1)S(1)} %bitcast.18), channel_id=1, replica_groups=mesh['xh'=2,'core'=2,'ctx'=32] {'xh','core','ctx'}, dimensions={0} | all-to-all | bytes 1048576 | tf_op jit(solution)/shard_map/all_to_all | solution.py:146
  89.1 0.9 %copy.10 = bf16[4,32,16,128]{3,1,2,0:T(8,128)(2,1)} copy(bf16[4,32,16,128]{3,2,1,0:T(8,128)(2,1)S(1)} %bitcast.21) | data formatting | bytes 1048576 | tf_op jit(solution)/shard_map/reshape | solution.py:149
Async XLA Ops:
  3.7 53.1 %copy-start = (f32[8,32,128]{2,1,0:T(8,128)S(1)}, f32[8,32,128]{2,1,0:T(8,128)}, u32[]{:S(2)}) copy-start(f32[8,32,128]{2,1,0:T(8,128)} %gates.1) | copy-start | bytes 393220
  3.7 53.1 %copy-start.1 = (s32[4,4]{1,0:T(4,128)S(1)}, s32[4,4]{1,0:T(4,128)}, u32[]{:S(2)}) copy-start(s32[4,4]{1,0:T(4,128)} %mask.1) | copy-start | bytes 196
  3.7 53.1 %copy-start.2 = (s32[4]{0:T(128)S(1)}, s32[4]{0:T(128)}, u32[]{:S(2)}) copy-start(s32[4]{0:T(128)} %order.1) | copy-start | bytes 52
  3.7 53.1 %copy-start.3 = (s32[4]{0:T(128)S(1)}, s32[4]{0:T(128)}, u32[]{:S(2)}) copy-start(s32[4]{0:T(128)} %levels.1) | copy-start | bytes 52
  49.7 7.1 %collective-permute-start = (bf16[64,160,128]{2,1,0:T(8,128)(2,1)S(1)}, bf16[64,160,128]{2,1,0:T(8,128)(2,1)}, u32[]{:S(2)}, u32[]{:S(2)}) collective-permute-start(bf16[64,160,128]{2,1,0:T(8,128)(2,1)S(1)} %all_to_all.10.own), channel_id=1, source_target_pairs={{0,32},{32,0},{1,33},{33,1},{2,34},{34,2},{3,35},{35,3},{4,36},{36... | collective-permute-start | bytes 7864328 | tf_op jit(solution)/shard_map/ppermute | solution.py:143

commit v3 on v1

v3 whole, which is shorter than its diff:
```python
import functools

import jax
import jax.numpy as jnp
from jax import lax
from jax.experimental import pallas as pl
from jax.experimental.pallas import tpu as pltpu
from jax.sharding import Mesh, PartitionSpec as P

LOG2E = 1.4426950408889634
SWAP = [(0, 1), (1, 0)]
BOTH = (((1,), (1,)), ((), ()))
TILE = 512
SMEM = pl.BlockSpec(memory_space=pltpu.SMEM)
VMEM = pl.BlockSpec(memory_space=pltpu.VMEM)
LIMIT = 48 * 2**20


def pack_kernel(queries, keys, values, send, q_in, k_in, v_in, wide, q_out, k_out, v_out, ins, outs):
    toks, heads, size = queries.shape
    half = toks // 2
    pitch = wide.shape[1] // toks
    parts = ((keys, k_in, k_out), (values, v_in, v_out), (queries, q_in, q_out))
    loads, stores = [], []
    for i, (src, dst, _) in enumerate(parts):
        for h in range(2):
            at = pl.ds(h * half, half)
            loads.append(pltpu.make_async_copy(src.at[at], dst.at[at], ins.at[2 * i + h]))
            loads[-1].start()
    for i, (_, part, turned) in enumerate(parts):
        for h in range(2):
            loads[2 * i + h].wait()
            for tok in range(h * half, (h + 1) * half):
                wide[i, tok * pitch : tok * pitch + heads, :] = part[tok].astype(jnp.float32)
        for head in range(heads):
            x = wide[i, pl.ds(head, toks, stride=pitch), :].astype(jnp.bfloat16)
            if i < 2:
                turned[head] = x
            else:
                turned[0, head] = x[:half]
                turned[1, head] = x[half:]
        for xh in range(2):
            src = turned if i < 2 else turned.at[xh]
            rows = pl.ds(i * toks, toks if i < 2 else half)
            dst = send.at[pl.ds(xh * heads, heads), rows]
            stores.append(pltpu.make_async_copy(src, dst, outs.at[2 * i + xh]))
            stores[-1].start()
    for copy in stores:
        copy.wait()


def pack(queries, keys, values):
    toks, heads, size = queries.shape
    hbm = pl.BlockSpec(memory_space=pl.ANY)
    block = pltpu.VMEM((toks, heads, size), jnp.bfloat16)
    turned = pltpu.VMEM((heads, toks, size), jnp.bfloat16)
    return pl.pallas_call(
        pack_kernel,
        out_shape=jax.ShapeDtypeStruct((2 * heads, 2 * toks + toks // 2, size), jnp.bfloat16),
        in_specs=[hbm, hbm, hbm],
        out_specs=hbm,
        scratch_shapes=[
            block,
            block,
            block,
            pltpu.VMEM((3, toks * (heads + 1), size), jnp.float32),
            pltpu.VMEM((2, heads, toks // 2, size), jnp.bfloat16),
            turned,
            turned,
            pltpu.SemaphoreType.DMA((6,)),
            pltpu.SemaphoreType.DMA((6,)),
        ],
        compiler_params=pltpu.CompilerParams(vmem_limit_bytes=60 * 2**20),
    )(queries, keys, values)


def stretch_of(slot, core):
    return 2 * (slot % 2) + jnp.where(slot < 2, core, 1 - core)


def load_slot(src, slot, core, toks, share, q_all, k_all):
    groups, size = src.shape[0] // 2, src.shape[-1]
    at = pl.ds((slot % 2) * groups, groups)
    start = pl.multiple_of(2 * toks + core * share, 16)
    q = src[at, pl.ds(start, share), :].reshape(groups * share, size).astype(jnp.float32)
    q = q * (LOG2E / size**0.5)
    high = q.astype(jnp.bfloat16)
    q_all[slot, :, 0:size] = high
    q_all[slot, :, size:] = (q - high.astype(jnp.float32)).astype(jnp.bfloat16)
    k_all[slot] = src[at, 0:toks, :].reshape(groups * toks, size)


def turn_values(src, slot, toks):
    groups, size = src.shape[0] // 2, src.shape[-1]
    row = lax.broadcasted_iota(jnp.int32, (size, size), 0)
    col = lax.broadcasted_iota(jnp.int32, (size, size), 1)
    eye = jnp.where(row == col, 1.0, 0.0).astype(jnp.bfloat16)
    v = src[pl.ds((slot % 2) * groups, groups), toks : 2 * toks, :].reshape(groups * toks, size)
    turned = lax.dot_general(eye, v, BOTH, preferred_element_type=jnp.float32)
    return turned.astype(jnp.bfloat16)


def run_pairs(slots, core, order, mask, pair_q, pair_k, q_all, k_all, v_all, state, bufs):
    run_max, total, mixed = state
    s_a, s_b, m_a, m_b, f_a, f_b = bufs
    keys, rows = s_a.shape
    count = jnp.int32(0)
    for query_slot, key_slot in slots:
        pair_q[count] = query_slot
        pair_k[count] = key_slot
        query_pos = order[stretch_of(query_slot, core)]
        key_pos = order[stretch_of(key_slot, core)]
        count = count + (mask[query_pos, key_pos] == 1).astype(jnp.int32)

    def step(n, s_new, m_new, f_new, s_old, m_old, f_old, used=True):
        later = jnp.minimum(n + 1, count - 1)
        next_q, next_k = pair_q[later], pair_k[later]
        q = q_all[next_q]
        best = sums = acc = None
        if used:
            now_q, now_k = pair_q[n], pair_k[n]
            m, f = m_old[0:1, :], f_old[0:1, :]
        for c in range(0, keys, TILE):
            k = k_all[next_k, c : c + TILE, :]
            s = lax.dot_general(
                jnp.concatenate([k, k], axis=1), q, BOTH, preferred_element_type=jnp.float32
            )
            s_new[c : c + TILE, :] = s
            top = jnp.max(s.reshape(TILE // 8, 8, rows), axis=0)
            best = top if best is None else jnp.maximum(best, top)
            if used:
                p = jnp.exp2(s_old[c : c + TILE, :] - m)
                t = jnp.sum(p.reshape(TILE // 8, 8, rows), axis=0)
                d = jnp.dot(
                    v_all[now_k, :, c : c + TILE],
                    p.astype(jnp.bfloat16),
                    preferred_element_type=jnp.float32,
                )
                sums = t if sums is None else sums + t
                acc = d if acc is None else acc + d
        if used:
            total[now_q] = total[now_q] * f + sums
            mixed[now_q] = mixed[now_q] * f + acc
        old = run_max[next_q]
        new = jnp.maximum(old, jnp.max(best, axis=0, keepdims=True))
        run_max[next_q] = new
        m_new[...] = new
        f_new[...] = jnp.exp2(old - new)

    a, b = (s_a, m_a, f_a), (s_b, m_b, f_b)
    step(-1, *a, *b, used=False)

    @pl.loop(0, (count + 1) // 2)
    def _(t):
        step(2 * t, *b, *a)

        @pl.when(2 * t + 1 < count)
        def _():
            step(2 * t + 1, *a, *b)


def clear(run_max, total, mixed):
    run_max[...] = jnp.full(run_max.shape, -1e30, jnp.float32)
    total[...] = jnp.zeros(total.shape, jnp.float32)
    mixed[...] = jnp.zeros(mixed.shape, jnp.float32)


def first_kernel(
    place, order, mask, own, run_max, total, mixed, v_all, pair_q, pair_k, q_all, k_all, *bufs, toks, share
):
    core = place[0]
    clear(run_max, total, mixed)
    for slot in range(2):
        load_slot(own, slot, core, toks, share, q_all, k_all)
        v_all[slot] = turn_values(own, slot, toks)
    slots = [(q, k) for q in range(2) for k in range(2)]
    state = (run_max, total, mixed)
    run_pairs(slots, core, order, mask, pair_q, pair_k, q_all, k_all, v_all, state, bufs)


def rest_kernel(
    place, order, levels, mask, own, other, gates, max_in, total_in, mixed_in, v_in, out,
    pair_q, pair_k, q_all, k_all, v_all, run_max, total, mixed, *bufs, toks, share
):
    core, head = place[0], place[1]
    clear(run_max.at[2:4], total.at[2:4], mixed.at[2:4])
    run_max[0:2] = max_in[...]
    total[0:2] = total_in[...]
    mixed[0:2] = mixed_in[...]
    v_all[0:2] = v_in[...]
    for slot in range(4):
        load_slot(own if slot < 2 else other, slot, core, toks, share, q_all, k_all)
        if slot >= 2:
            v_all[slot] = turn_values(other, slot, toks)
    slots = [(q, k) for k in range(4) for q in range(4) if q >= 2 or k >= 2]
    state = (run_max, total, mixed)
    run_pairs(slots, core, order, mask, pair_q, pair_k, q_all, k_all, v_all, state, bufs)
    groups, size = own.shape[0] // 2, own.shape[-1]
    for slot in range(4):
        stretch = stretch_of(slot, core)
        gate = gates[levels[stretch], pl.ds(head, 1), :]
        o = mixed[slot] / jnp.sum(total[slot], axis=0, keepdims=True)
        out[stretch] = (o.T * gate).astype(jnp.bfloat16).reshape(groups, share, size)


def state_of(n, rows, size):
    return [(n, 8, rows), (n, 8, rows), (n, size, rows)]


def scratch(n, rows, keys, size):
    f32, bf16 = jnp.float32, jnp.bfloat16
    head = [
        pltpu.SMEM((17,), jnp.int32),
        pltpu.SMEM((17,), jnp.int32),
        pltpu.VMEM((n, rows, 2 * size), bf16),
        pltpu.VMEM((n, keys, size), bf16),
    ]
    bufs = [pltpu.VMEM((keys, rows), f32)] * 2 + [pltpu.VMEM((8, rows), f32)] * 4
    return head, bufs


def first(place, order, mask, own, toks, share):
    groups, size = own.shape[0] // 2, own.shape[-1]
    rows, keys = groups * share, groups * toks
    head, bufs = scratch(2, rows, keys, size)
    shapes = [jax.ShapeDtypeStruct(s, jnp.float32) for s in state_of(2, rows, size)]
    shapes.append(jax.ShapeDtypeStruct((2, size, keys), jnp.bfloat16))
    return pl.pallas_call(
        functools.partial(first_kernel, toks=toks, share=share),
        out_shape=shapes,
        in_specs=[SMEM, SMEM, SMEM, VMEM],
        out_specs=[VMEM] * 4,
        scratch_shapes=head + bufs,
        compiler_params=pltpu.CompilerParams(vmem_limit_bytes=LIMIT),
        cost_estimate=pl.CostEstimate(
            flops=3 * 4 * rows * keys * size,
            bytes_accessed=8 * 2**20,
            transcendentals=3 * rows * keys,
        ),
    )(place, order, mask, own)


def rest(place, order, levels, mask, own, other, gates, state, toks, share):
    groups, size = own.shape[0] // 2, own.shape[-1]
    rows, keys = groups * share, groups * toks
    head, bufs = scratch(4, rows, keys, size)
    mine = [pltpu.VMEM((4, size, keys), jnp.bfloat16)]
    mine += [pltpu.VMEM(s, jnp.float32) for s in state_of(4, rows, size)]
    return pl.pallas_call(
        functools.partial(rest_kernel, toks=toks, share=share),
        out_shape=jax.ShapeDtypeStruct((4, groups, share, size), jnp.bfloat16),
        in_specs=[SMEM] * 4 + [VMEM] * 7,
        out_specs=VMEM,
        scratch_shapes=head + mine + bufs,
        compiler_params=pltpu.CompilerParams(vmem_limit_bytes=LIMIT),
    )(place, order, levels, mask, own, other, gates, *state)


def shards(queries, keys, values, gate_table, noise_level, stretch_order, block_mask):
    toks, heads, size = queries.shape[1:]
    share = toks // 4
    own = lax.all_to_all(pack(queries[0], keys[0], values[0]), ("xh", "ctx"), 0, 0, tiled=True)
    other = lax.ppermute(own, "core", SWAP)
    place = jnp.stack([lax.axis_index("core"), lax.axis_index("ctx")]).astype(jnp.int32)
    state = first(place, stretch_order, block_mask, own, toks, share)
    part = rest(
        place, stretch_order, noise_level, block_mask, own, other, gate_table, state, toks, share
    )
    back = lax.all_to_all(
        part.reshape(4 * heads, share, size), ("xh", "core", "ctx"), 0, 0, tiled=True
    )
    back = back.reshape(4, heads, share, size)
    return jnp.swapaxes(back, 1, 2).reshape(1, toks, heads, size)


def solution(mesh):
    wide = Mesh(mesh.devices.reshape(2, 2, -1), ("xh", "core", "ctx"))
    tokens = P(("xh", "core"), "ctx", None, None)
    return jax.shard_map(
        shards,
        mesh=wide,
        in_specs=(tokens, tokens, tokens, P(), P(), P(), P()),
        out_specs=tokens,
        check_vma=False,
    )
```

time: 95.8 us -> 85.4 us (0.89)
  waiting for transfers between devices: 4.59 us -> 0.27 us
  Pallas kernels: 19.2 us -> 16.9 us
  local copies, waits for them, and re-layouts: 3.1 us -> 0.95 us
  other arithmetic: 1.57 us -> 0.07 us
    ppermute x1, waiting for transfers between devices: 4.59 us -> 0.27 us  [shards(): other = lax.ppermute(own, 'core', SWAP)]
    pallas_call x1 -> x3, Pallas kernels: 19.2 us -> 16.9 us  [the longest x1 9.89 us: rest(): pl.pallas_call(functools.partial(rest_kernel, toks=toks, share=share), ou...]
    concatenate x2 -> x0, other arithmetic: 1.49 us -> none  [the longest x1 1.29 us: shards(): kv = jnp.concatenate([k, v], axis=1)]
    another operation x1 -> x0, local copies, waits for them, and re-layouts: 1.25 us -> none  [shards(): q = jnp.swapaxes(queries[0].reshape(2, half, heads, size), 1, 2)]
  transfers between devices with their start and end apart: 1 -> 1, of which waited for: 1 -> 1; matrix products, arithmetic and copies ran while one was open for 0% -> 0% of each run, Pallas kernels for 0% -> 5%
where the time goes in v3:
time: 85.4 us; the launch traced here: 84.1 us
  blocking collectives  63.3 us (74%)
  Pallas kernels  16.9 us (20%)
  starting transfers between devices  2.46 us (3%)
  local copies, waits for them, and re-layouts  0.95 us (1%)
    all_to_all x1, blocking collectives, shards(): lax.all_to_all(pack(queries[0], keys[0], values[0]), ('xh', 'ctx'), 0, 0,...  46 us
    all_to_all x1, blocking collectives, shards(): lax.all_to_all(part.reshape(4 * heads, share, size), ('xh', 'core', 'ctx'...  17.3 us
    pallas_call x1, Pallas kernels, rest(): pl.pallas_call(functools.partial(rest_kernel, toks=toks, share=share), ou...  9.89 us
    pallas_call x1, Pallas kernels, first(): pl.pallas_call(functools.partial(first_kernel, toks=toks, share=share), o...  4.3 us
    pallas_call x1, Pallas kernels, pack(): pl.pallas_call(pack_kernel, out_shape=jax.ShapeDtypeStruct((2 * heads, 2...  2.73 us
    ppermute x1, starting transfers between devices, shards(): other = lax.ppermute(own, 'core', SWAP)  2.46 us
  transfers between devices with their start and end apart: 1, of which 1 were waited for; matrix products, arithmetic and copies ran while one was open for 0% of the time, Pallas kernels for 5%

profile of v3, /device:TPU:1, one launch (start us, length us, event | category | flops | bytes accessed | tf_op | source)
XLA Modules:
  0.0 84.1 jit_solution(7621683966206880013)
XLA Ops:
  0.0 2.7 %shard_map.73 = bf16[64,160,128]{2,1,0:T(8,128)(2,1)} custom-call(bf16[64,32,128]{2,1,0:T(8,128)(2,1)} %bitcast.12, bf16[64,32,128]{2,1,0:T(8,128)(2,1)} %bitcast.13, bf16[64,32,128]{2,1,0:T(8,128)(2,1)} %bitcast.14), custom_call_target="tpu_custom_call" | custom-call | tf_op jit(solution)/shard_map/pallas_call | solution.py:57
  2.7 0.0 copy-start.1
  2.7 0.0 copy-start.2
  2.8 46.0 %all_to_all.10.own = bf16[64,160,128]{2,1,0:T(8,128)(2,1)S(1)} all-to-all(bf16[64,160,128]{2,1,0:T(8,128)(2,1)} %shard_map.73), channel_id=1, replica_groups=mesh['xh'=2,'core'=2,'ctx'=32] {'xh','ctx'}, dimensions={0} | all-to-all | bytes 5242880 | tf_op jit(solution)/shard_map/all_to_all | solution.py:262
  48.8 2.5 %collective-permute-start = (bf16[64,160,128]{2,1,0:T(8,128)(2,1)S(1)}, bf16[64,160,128]{2,1,0:T(8,128)(2,1)}, u32[]{:S(2)}, u32[]{:S(2)}) collective-permute-start(bf16[64,160,128]{2,1,0:T(8,128)(2,1)S(1)} %all_to_all.10.own), channel_id=1, source_target_pairs={{0,32},{32,0},{1,33},{33,1},{2,34},{34,2},{3,35},{35,3},{4,36},{36... | collective-permute-start | bytes 7864328 | tf_op jit(solution)/shard_map/ppermute | solution.py:263
  51.3 0.1 pad_add_fusion.place
  51.3 0.0 copy-done.1
  51.3 0.0 copy-done.2
  51.3 0.0 copy-start
  51.3 0.0 copy-start.3
  51.3 4.3 %shard_map.74 = (f32[2,8,512]{2,1,0:T(8,128)S(1)}, f32[2,8,512]{2,1,0:T(8,128)S(1)}, f32[2,128,512]{2,1,0:T(8,128)S(1)}, bf16[2,128,2048]{2,1,0:T(8,128)(2,1)S(1)}) custom-call(s32[2]{0:T(128)S(1)} %pad_add_fusion.place, s32[4]{0:T(128)S(1)} %copy-done.2, s32[4,4]{1,0:T(4,128)S(1)} %copy-done.1, bf16[64,160,128]{2,1,0:T(8,128)(2,1)S(1)} %all_to_all.10.own), custom_call_target="tpu_custom_call" | custom-call | flops 1610612736 | bytes 8388608 | tf_op jit(solution)/shard_map/pallas_call | solution.py:228
  55.7 0.3 collective-permute-done.other
  55.9 0.0 copy-done
  55.9 0.0 copy-done.3
  55.9 9.9 %shard_map.75 = bf16[4,32,16,128]{3,2,1,0:T(8,128)(2,1)S(1)} custom-call(s32[2]{0:T(128)S(1)} %pad_add_fusion.place, s32[4]{0:T(128)S(1)} %copy-done.2, s32[4]{0:T(128)S(1)} %copy-done.3, s32[4,4]{1,0:T(4,128)S(1)} %copy-done.1, bf16[64,160,128]{2,1,0:T(8,128)(2,1)S(1)} %all_to_all.10.own, bf16[64,160,128]{2,1,0:T(8,128)(2,1)} %collective-permute-done.other, ...), custom_call_target="tpu_custom_call" | custom-call | tf_op jit(solution)/shard_map/pallas_call | solution.py:249
  65.8 17.3 %all_to_all.11 = bf16[128,16,128]{2,1,0:T(8,128)(2,1)S(1)} all-to-all(bf16[128,16,128]{2,1,0:T(8,128)(2,1)S(1)} %bitcast.10), channel_id=1, replica_groups=mesh['xh'=2,'core'=2,'ctx'=32] {'xh','core','ctx'}, dimensions={0} | all-to-all | bytes 1048576 | tf_op jit(solution)/shard_map/all_to_all | solution.py:269
  83.1 0.9 %copy.8 = bf16[4,32,16,128]{3,1,2,0:T(8,128)(2,1)} copy(bf16[4,32,16,128]{3,2,1,0:T(8,128)(2,1)S(1)} %bitcast.11) | data formatting | bytes 1048576 | tf_op jit(solution)/shard_map/reshape | solution.py:272
Async XLA Ops:
  2.7 48.6 %copy-start.1 = (s32[4,4]{1,0:T(4,128)S(1)}, s32[4,4]{1,0:T(4,128)}, u32[]{:S(2)}) copy-start(s32[4,4]{1,0:T(4,128)} %mask.3) | copy-start | bytes 196
  2.7 48.6 %copy-start.2 = (s32[4]{0:T(128)S(1)}, s32[4]{0:T(128)}, u32[]{:S(2)}) copy-start(s32[4]{0:T(128)} %order.3) | copy-start | bytes 52
  48.8 7.1 %collective-permute-start = (bf16[64,160,128]{2,1,0:T(8,128)(2,1)S(1)}, bf16[64,160,128]{2,1,0:T(8,128)(2,1)}, u32[]{:S(2)}, u32[]{:S(2)}) collective-permute-start(bf16[64,160,128]{2,1,0:T(8,128)(2,1)S(1)} %all_to_all.10.own), channel_id=1, source_target_pairs={{0,32},{32,0},{1,33},{33,1},{2,34},{34,2},{3,35},{35,3},{4,36},{36... | collective-permute-start | bytes 7864328 | tf_op jit(solution)/shard_map/ppermute | solution.py:263
  51.3 4.6 %copy-start = (f32[8,32,128]{2,1,0:T(8,128)S(1)}, f32[8,32,128]{2,1,0:T(8,128)}, u32[]{:S(2)}) copy-start(f32[8,32,128]{2,1,0:T(8,128)} %gates.1) | copy-start | bytes 393220
  51.3 4.6 %copy-start.3 = (s32[4]{0:T(128)S(1)}, s32[4]{0:T(128)}, u32[]{:S(2)}) copy-start(s32[4]{0:T(128)} %levels.1) | copy-start | bytes 52

commit v4 on v3

--- a/solution.py
+++ b/solution.py
@@ -78,57 +78,53 @@
     return 2 * (slot % 2) + jnp.where(slot < 2, core, 1 - core)
 
 
-def load_slot(src, slot, core, toks, share, q_all, k_all):
-    groups, size = src.shape[0] // 2, src.shape[-1]
-    at = pl.ds((slot % 2) * groups, groups)
-    start = pl.multiple_of(2 * toks + core * share, 16)
-    q = src[at, pl.ds(start, share), :].reshape(groups * share, size).astype(jnp.float32)
-    q = q * (LOG2E / size**0.5)
+def load_queries(q, slot, q_all):
+    groups, share, size = q.shape
+    q = q.reshape(groups * share, size).astype(jnp.float32) * (LOG2E / size**0.5)
     high = q.astype(jnp.bfloat16)
     q_all[slot, :, 0:size] = high
     q_all[slot, :, size:] = (q - high.astype(jnp.float32)).astype(jnp.bfloat16)
-    k_all[slot] = src[at, 0:toks, :].reshape(groups * toks, size)
-
-
-def turn_values(src, slot, toks):
-    groups, size = src.shape[0] // 2, src.shape[-1]
-    row = lax.broadcasted_iota(jnp.int32, (size, size), 0)
-    col = lax.broadcasted_iota(jnp.int32, (size, size), 1)
-    eye = jnp.where(row == col, 1.0, 0.0).astype(jnp.bfloat16)
-    v = src[pl.ds((slot % 2) * groups, groups), toks : 2 * toks, :].reshape(groups * toks, size)
-    turned = lax.dot_general(eye, v, BOTH, preferred_element_type=jnp.float32)
-    return turned.astype(jnp.bfloat16)
-
-
-def run_pairs(slots, core, order, mask, pair_q, pair_k, q_all, k_all, v_all, state, bufs):
+
+
+def load_own(own, core, toks, share, q_all, k_all):
+    groups = own.shape[0] // 2
+    start = pl.multiple_of(2 * toks + core * share, 16)
+    for slot in range(2):
+        at = slice(slot * groups, (slot + 1) * groups)
+        load_queries(own[at, pl.ds(start, share), :], slot, q_all)
+        k_all[slot] = own[at, 0:toks, :]
+
+
+def turn(v):
+    groups, toks, size = v.shape
+    return v.reshape(groups * toks, size).T
+
+
+def make_step(q_all, k_all, v_all, state, keys):
     run_max, total, mixed = state
-    s_a, s_b, m_a, m_b, f_a, f_b = bufs
-    keys, rows = s_a.shape
-    count = jnp.int32(0)
-    for query_slot, key_slot in slots:
-        pair_q[count] = query_slot
-        pair_k[count] = key_slot
-        query_pos = order[stretch_of(query_slot, core)]
-        key_pos = order[stretch_of(key_slot, core)]
-        count = count + (mask[query_pos, key_pos] == 1).astype(jnp.int32)
-
-    def step(n, s_new, m_new, f_new, s_old, m_old, f_old, used=True):
-        later = jnp.minimum(n + 1, count - 1)
-        next_q, next_k = pair_q[later], pair_k[later]
-        q = q_all[next_q]
+    rows, size = q_all.shape[1], k_all.shape[-1]
+    toks = k_all.shape[2]
+
+    def step(fresh, new, used, old):
         best = sums = acc = None
-        if used:
-            now_q, now_k = pair_q[n], pair_k[n]
+        if used is not None:
+            s_old, m_old, f_old = old
+            now_q, now_k = used
             m, f = m_old[0:1, :], f_old[0:1, :]
+        if fresh is not None:
+            s_new, m_new, f_new = new
+            next_q, next_k = fresh
+            q = q_all[next_q]
         for c in range(0, keys, TILE):
-            k = k_all[next_k, c : c + TILE, :]
-            s = lax.dot_general(
-                jnp.concatenate([k, k], axis=1), q, BOTH, preferred_element_type=jnp.float32
-            )
-            s_new[c : c + TILE, :] = s
-            top = jnp.max(s.reshape(TILE // 8, 8, rows), axis=0)
-            best = top if best is None else jnp.maximum(best, top)
-            if used:
+            if fresh is not None:
+                k = k_all[next_k, c // toks : (c + TILE) // toks].reshape(TILE, size)
+                s = lax.dot_general(
+                    jnp.concatenate([k, k], axis=1), q, BOTH, preferred_element_type=jnp.float32
+                )
+                s_new[c : c + TILE, :] = s
+                top = jnp.max(s.reshape(TILE // 8, 8, rows), axis=0)
+                best = top if best is None else jnp.maximum(best, top)
+            if used is not None:
                 p = jnp.exp2(s_old[c : c + TILE, :] - m)
                 t = jnp.sum(p.reshape(TILE // 8, 8, rows), axis=0)
                 d = jnp.dot(
@@ -138,25 +134,17 @@
                 )
                 sums = t if sums is None else sums + t
                 acc = d if acc is None else acc + d
-        if used:
+        if used is not None:
             total[now_q] = total[now_q] * f + sums
             mixed[now_q] = mixed[now_q] * f + acc
-        old = run_max[next_q]
-        new = jnp.maximum(old, jnp.max(best, axis=0, keepdims=True))
-        run_max[next_q] = new
-        m_new[...] = new
-        f_new[...] = jnp.exp2(old - new)
-
-    a, b = (s_a, m_a, f_a), (s_b, m_b, f_b)
-    step(-1, *a, *b, used=False)
-
-    @pl.loop(0, (count + 1) // 2)
-    def _(t):
-        step(2 * t, *b, *a)
-
-        @pl.when(2 * t + 1 < count)
-        def _():
-            step(2 * t + 1, *a, *b)
+        if fresh is not None:
+            before = run_max[next_q]
+            after = jnp.maximum(before, jnp.max(best, axis=0, keepdims=True))
+            run_max[next_q] = after
+            m_new[...] = after
+            f_new[...] = jnp.exp2(before - after)
+
+    return step
 
 
 def clear(run_max, total, mixed):
@@ -166,36 +154,104 @@
 
 
 def first_kernel(
-    place, order, mask, own, run_max, total, mixed, v_all, pair_q, pair_k, q_all, k_all, *bufs, toks, share
+    place, order, mask, own, run_max, total, mixed, v_all, q_all, k_all, *bufs, toks, share
 ):
     core = place[0]
+    groups = own.shape[0] // 2
     clear(run_max, total, mixed)
-    for slot in range(2):
-        load_slot(own, slot, core, toks, share, q_all, k_all)
-        v_all[slot] = turn_values(own, slot, toks)
-    slots = [(q, k) for q in range(2) for k in range(2)]
-    state = (run_max, total, mixed)
-    run_pairs(slots, core, order, mask, pair_q, pair_k, q_all, k_all, v_all, state, bufs)
+    load_own(own, core, toks, share, q_all, k_all)
+    step = make_step(q_all, k_all, v_all, (run_max, total, mixed), groups * toks)
+    a, b = bufs[0::2], bufs[1::2]
+    step((0, 0), a, None, None)
+    for slot in range(2):
+        v_all[slot] = turn(own[slot * groups : (slot + 1) * groups, toks : 2 * toks, :])
+    step((1, 1), b, (0, 0), a)
+    here, there = order[stretch_of(0, core)], order[stretch_of(1, core)]
+    later = jnp.where(here > there, 0, 1)
+    cross = (later, 1 - later)
+    crossed = mask[jnp.maximum(here, there), jnp.minimum(here, there)] == 1
+
+    @pl.when(crossed)
+    def _():
+        step(cross, a, (1, 1), b)
+        step(None, None, cross, a)
+
+    @pl.when(jnp.logical_not(crossed))
+    def _():
+        step(None, None, (1, 1), b)
 
 
 def rest_kernel(
     place, order, levels, mask, own, other, gates, max_in, total_in, mixed_in, v_in, out,
-    pair_q, pair_k, q_all, k_all, v_all, run_max, total, mixed, *bufs, toks, share
+    pair_q, pair_k, sems, q_raw, v_raw, q_all, k_all, v_all, run_max, total, mixed, *bufs, toks, share
 ):
     core, head = place[0], place[1]
+    groups, size = own.shape[0] // 2, own.shape[-1]
+    start = pl.multiple_of(2 * toks + core * share, 16)
+    copies = []
+    for slot in range(2):
+        at = pl.ds(slot * groups, groups)
+        for rows, dst in (
+            (pl.ds(0, toks), k_all.at[2 + slot]),
+            (pl.ds(start, share), q_raw.at[slot]),
+            (pl.ds(toks, toks), v_raw.at[slot]),
+        ):
+            copy = pltpu.make_async_copy(other.at[at, rows], dst, sems.at[len(copies)])
+            copy.start()
+            copies.append(copy)
     clear(run_max.at[2:4], total.at[2:4], mixed.at[2:4])
     run_max[0:2] = max_in[...]
     total[0:2] = total_in[...]
     mixed[0:2] = mixed_in[...]
     v_all[0:2] = v_in[...]
-    for slot in range(4):
-        load_slot(own if slot < 2 else other, slot, core, toks, share, q_all, k_all)
-        if slot >= 2:
-            v_all[slot] = turn_values(other, slot, toks)
-    slots = [(q, k) for k in range(4) for q in range(4) if q >= 2 or k >= 2]
-    state = (run_max, total, mixed)
-    run_pairs(slots, core, order, mask, pair_q, pair_k, q_all, k_all, v_all, state, bufs)
-    groups, size = own.shape[0] // 2, own.shape[-1]
+    load_own(own, core, toks, share, q_all, k_all)
+
+    count = jnp.int32(0)
+    slots = [(2, 2)] + [(q, k) for k in range(4) for q in range(4) if max(q, k) > 1]
+    for i, (query_slot, key_slot) in enumerate(slots):
+        pair_q[count] = query_slot
+        pair_k[count] = key_slot
+        query_pos = order[stretch_of(query_slot, core)]
+        key_pos = order[stretch_of(key_slot, core)]
+        fits = mask[query_pos, key_pos] == 1
+        if i == 0:
+            fits = jnp.bool_(True)
+        elif (query_slot, key_slot) == (2, 2):
+            fits = jnp.bool_(False)
+        count = count + fits.astype(jnp.int32)
+
+    step = make_step(q_all, k_all, v_all, (run_max, total, mixed), groups * toks)
+    a, b = bufs[0::2], bufs[1::2]
+
+    def pair(n):
+        return pair_q[n], pair_k[n]
+
+    for slot in range(2):
+        copies[3 * slot].wait()
+        copies[3 * slot + 1].wait()
+        load_queries(q_raw[slot], 2 + slot, q_all)
+    for slot in range(2):
+        copies[3 * slot + 2].wait()
+    step((2, 2), a, None, None)
+    for slot in range(2):
+        v_all[2 + slot] = turn(v_raw[slot])
+
+    steps = count - 1
+
+    @pl.loop(0, steps // 2)
+    def _(t):
+        step(pair(2 * t + 1), b, pair(2 * t), a)
+        step(pair(2 * t + 2), a, pair(2 * t + 1), b)
+
+    @pl.when(steps % 2 == 1)
+    def _():
+        step(pair(steps), b, pair(steps - 1), a)
+        step(None, None, pair(steps), b)
+
+    @pl.when(steps % 2 == 0)
+    def _():
+        step(None, None, pair(steps), a)
+
     for slot in range(4):
         stretch = stretch_of(slot, core)
         gate = gates[levels[stretch], pl.ds(head, 1), :]
@@ -207,14 +263,10 @@
     return [(n, 8, rows), (n, 8, rows), (n, size, rows)]
 
 
-def scratch(n, rows, keys, size):
+def scratch(n, groups, toks, share, size):
     f32, bf16 = jnp.float32, jnp.bfloat16
-    head = [
-        pltpu.SMEM((17,), jnp.int32),
-        pltpu.SMEM((17,), jnp.int32),
-        pltpu.VMEM((n, rows, 2 * size), bf16),
-        pltpu.VMEM((n, keys, size), bf16),
-    ]
+    rows, keys = groups * share, groups * toks
+    head = [pltpu.VMEM((n, rows, 2 * size), bf16), pltpu.VMEM((n, groups, toks, size), bf16)]
     bufs = [pltpu.VMEM((keys, rows), f32)] * 2 + [pltpu.VMEM((8, rows), f32)] * 4
     return head, bufs
 
@@ -222,7 +274,7 @@
 def first(place, order, mask, own, toks, share):
     groups, size = own.shape[0] // 2, own.shape[-1]
     rows, keys = groups * share, groups * toks
-    head, bufs = scratch(2, rows, keys, size)
+    head, bufs = scratch(2, groups, toks, share, size)
     shapes = [jax.ShapeDtypeStruct(s, jnp.float32) for s in state_of(2, rows, size)]
     shapes.append(jax.ShapeDtypeStruct((2, size, keys), jnp.bfloat16))
     return pl.pallas_call(
@@ -243,15 +295,22 @@
 def rest(place, order, levels, mask, own, other, gates, state, toks, share):
     groups, size = own.shape[0] // 2, own.shape[-1]
     rows, keys = groups * share, groups * toks
-    head, bufs = scratch(4, rows, keys, size)
+    head, bufs = scratch(4, groups, toks, share, size)
+    lists = [
+        pltpu.SMEM((17,), jnp.int32),
+        pltpu.SMEM((17,), jnp.int32),
+        pltpu.SemaphoreType.DMA((6,)),
+        pltpu.VMEM((2, groups, share, size), jnp.bfloat16),
+        pltpu.VMEM((2, groups, toks, size), jnp.bfloat16),
+    ]
     mine = [pltpu.VMEM((4, size, keys), jnp.bfloat16)]
     mine += [pltpu.VMEM(s, jnp.float32) for s in state_of(4, rows, size)]
     return pl.pallas_call(
         functools.partial(rest_kernel, toks=toks, share=share),
         out_shape=jax.ShapeDtypeStruct((4, groups, share, size), jnp.bfloat16),
-        in_specs=[SMEM] * 4 + [VMEM] * 7,
+        in_specs=[SMEM] * 4 + [VMEM, pl.BlockSpec(memory_space=pl.ANY)] + [VMEM] * 5,
         out_specs=VMEM,
-        scratch_shapes=head + mine + bufs,
+        scratch_shapes=lists + head + mine + bufs,
         compiler_params=pltpu.CompilerParams(vmem_limit_bytes=LIMIT),
     )(place, order, levels, mask, own, other, gates, *state)
 

time: 85.4 us -> 85.3 us (level)
  transfers between devices with their start and end apart: 1 -> 1, of which waited for: 1 -> 0; matrix products, arithmetic and copies ran while one was open for 0% -> 0% of each run, Pallas kernels for 5% -> 5%
where the time goes in v4:
time: 85.3 us; the launch traced here: 84.4 us
  blocking collectives  63.3 us (74%)
  Pallas kernels  17.6 us (21%)
  starting transfers between devices  2.46 us (3%)
  local copies, waits for them, and re-layouts  0.95 us (1%)
    all_to_all x1, blocking collectives, shards(): lax.all_to_all(pack(queries[0], keys[0], values[0]), ('xh', 'ctx'), 0, 0,...  46 us
    all_to_all x1, blocking collectives, shards(): lax.all_to_all(part.reshape(4 * heads, share, size), ('xh', 'core', 'ctx'...  17.3 us
    pallas_call x1, Pallas kernels, rest(): pl.pallas_call(functools.partial(rest_kernel, toks=toks, share=share), ou...  10.2 us
    pallas_call x1, Pallas kernels, first(): pl.pallas_call(functools.partial(first_kernel, toks=toks, share=share), o...  4.59 us
    pallas_call x1, Pallas kernels, pack(): pl.pallas_call(pack_kernel, out_shape=jax.ShapeDtypeStruct((2 * heads, 2...  2.73 us
    ppermute x1, starting transfers between devices, shards(): other = lax.ppermute(own, 'core', SWAP)  2.46 us
  transfers between devices with their start and end apart: 1, of which 0 were waited for; matrix products, arithmetic and copies ran while one was open for 0% of the time, Pallas kernels for 5%

profile of v4, /device:TPU:1, one launch (start us, length us, event | category | flops | bytes accessed | tf_op | source)
XLA Modules:
  0.0 84.4 jit_solution(3912464906443204354)
XLA Ops:
  0.0 2.7 %shard_map.73 = bf16[64,160,128]{2,1,0:T(8,128)(2,1)} custom-call(bf16[64,32,128]{2,1,0:T(8,128)(2,1)} %bitcast.12, bf16[64,32,128]{2,1,0:T(8,128)(2,1)} %bitcast.13, bf16[64,32,128]{2,1,0:T(8,128)(2,1)} %bitcast.14), custom_call_target="tpu_custom_call" | custom-call | tf_op jit(solution)/shard_map/pallas_call | solution.py:57
  2.7 0.0 copy-start.1
  2.7 0.0 copy-start.2
  2.8 46.0 %all_to_all.10.own = bf16[64,160,128]{2,1,0:T(8,128)(2,1)S(1)} all-to-all(bf16[64,160,128]{2,1,0:T(8,128)(2,1)} %shard_map.73), channel_id=1, replica_groups=mesh['xh'=2,'core'=2,'ctx'=32] {'xh','ctx'}, dimensions={0} | all-to-all | bytes 5242880 | tf_op jit(solution)/shard_map/all_to_all | solution.py:321
  48.8 2.5 %collective-permute-start = (bf16[64,160,128]{2,1,0:T(8,128)(2,1)S(1)}, bf16[64,160,128]{2,1,0:T(8,128)(2,1)}, u32[]{:S(2)}, u32[]{:S(2)}) collective-permute-start(bf16[64,160,128]{2,1,0:T(8,128)(2,1)S(1)} %all_to_all.10.own), channel_id=1, source_target_pairs={{0,32},{32,0},{1,33},{33,1},{2,34},{34,2},{3,35},{35,3},{4,36},{36... | collective-permute-start | bytes 7864328 | tf_op jit(solution)/shard_map/ppermute | solution.py:322
  51.3 0.1 pad_add_fusion.place
  51.3 0.0 copy-done.1
  51.3 0.0 copy-done.2
  51.3 0.0 copy-start
  51.3 0.0 copy-start.3
  51.3 4.6 %shard_map.74 = (f32[2,8,512]{2,1,0:T(8,128)S(1)}, f32[2,8,512]{2,1,0:T(8,128)S(1)}, f32[2,128,512]{2,1,0:T(8,128)S(1)}, bf16[2,128,2048]{2,1,0:T(8,128)(2,1)S(1)}) custom-call(s32[2]{0:T(128)S(1)} %pad_add_fusion.place, s32[4]{0:T(128)S(1)} %copy-done.2, s32[4,4]{1,0:T(4,128)S(1)} %copy-done.1, bf16[64,160,128]{2,1,0:T(8,128)(2,1)S(1)} %all_to_all.10.own), custom_call_target="tpu_custom_call" | custom-call | flops 1610612736 | bytes 8388608 | tf_op jit(solution)/shard_map/pallas_call | solution.py:280
  55.9 0.0 collective-permute-done.other
  56.0 0.0 copy-done
  56.0 0.0 copy-done.3
  56.0 10.2 %shard_map.75 = bf16[4,32,16,128]{3,2,1,0:T(8,128)(2,1)S(1)} custom-call(s32[2]{0:T(128)S(1)} %pad_add_fusion.place, s32[4]{0:T(128)S(1)} %copy-done.2, s32[4]{0:T(128)S(1)} %copy-done.3, s32[4,4]{1,0:T(4,128)S(1)} %copy-done.1, bf16[64,160,128]{2,1,0:T(8,128)(2,1)S(1)} %all_to_all.10.own, bf16[64,160,128]{2,1,0:T(8,128)(2,1)} %collective-permute-done.other, ...), custom_call_target="tpu_custom_call" | custom-call | tf_op jit(solution)/shard_map/pallas_call | solution.py:308
  66.2 17.3 %all_to_all.11 = bf16[128,16,128]{2,1,0:T(8,128)(2,1)S(1)} all-to-all(bf16[128,16,128]{2,1,0:T(8,128)(2,1)S(1)} %bitcast.10), channel_id=1, replica_groups=mesh['xh'=2,'core'=2,'ctx'=32] {'xh','core','ctx'}, dimensions={0} | all-to-all | bytes 1048576 | tf_op jit(solution)/shard_map/all_to_all | solution.py:328
  83.5 0.9 %copy.8 = bf16[4,32,16,128]{3,1,2,0:T(8,128)(2,1)} copy(bf16[4,32,16,128]{3,2,1,0:T(8,128)(2,1)S(1)} %bitcast.11) | data formatting | bytes 1048576 | tf_op jit(solution)/shard_map/reshape | solution.py:331
Async XLA Ops:
  2.7 48.6 %copy-start.1 = (s32[4,4]{1,0:T(4,128)S(1)}, s32[4,4]{1,0:T(4,128)}, u32[]{:S(2)}) copy-start(s32[4,4]{1,0:T(4,128)} %mask.3) | copy-start | bytes 196
  2.7 48.6 %copy-start.2 = (s32[4]{0:T(128)S(1)}, s32[4]{0:T(128)}, u32[]{:S(2)}) copy-start(s32[4]{0:T(128)} %order.3) | copy-start | bytes 52
  48.8 7.2 %collective-permute-start = (bf16[64,160,128]{2,1,0:T(8,128)(2,1)S(1)}, bf16[64,160,128]{2,1,0:T(8,128)(2,1)}, u32[]{:S(2)}, u32[]{:S(2)}) collective-permute-start(bf16[64,160,128]{2,1,0:T(8,128)(2,1)S(1)} %all_to_all.10.own), channel_id=1, source_target_pairs={{0,32},{32,0},{1,33},{33,1},{2,34},{34,2},{3,35},{35,3},{4,36},{36... | collective-permute-start | bytes 7864328 | tf_op jit(solution)/shard_map/ppermute | solution.py:322
  51.3 4.6 %copy-start = (f32[8,32,128]{2,1,0:T(8,128)S(1)}, f32[8,32,128]{2,1,0:T(8,128)}, u32[]{:S(2)}) copy-start(f32[8,32,128]{2,1,0:T(8,128)} %gates.1) | copy-start | bytes 393220
  51.3 4.6 %copy-start.3 = (s32[4]{0:T(128)S(1)}, s32[4]{0:T(128)}, u32[]{:S(2)}) copy-start(s32[4]{0:T(128)} %levels.1) | copy-start | bytes 52

commit v5 on v4

--- a/solution.py
+++ b/solution.py
@@ -80,10 +80,7 @@
 
 def load_queries(q, slot, q_all):
     groups, share, size = q.shape
-    q = q.reshape(groups * share, size).astype(jnp.float32) * (LOG2E / size**0.5)
-    high = q.astype(jnp.bfloat16)
-    q_all[slot, :, 0:size] = high
-    q_all[slot, :, size:] = (q - high.astype(jnp.float32)).astype(jnp.bfloat16)
+    q_all[slot] = q.reshape(groups * share, size)
 
 
 def load_own(own, core, toks, share, q_all, k_all):
@@ -104,9 +101,10 @@
     run_max, total, mixed = state
     rows, size = q_all.shape[1], k_all.shape[-1]
     toks = k_all.shape[2]
+    scale = LOG2E / size**0.5
 
     def step(fresh, new, used, old):
-        best = sums = acc = None
+        best = acc = None
         if used is not None:
             s_old, m_old, f_old = old
             now_q, now_k = used
@@ -119,30 +117,28 @@
             if fresh is not None:
                 k = k_all[next_k, c // toks : (c + TILE) // toks].reshape(TILE, size)
                 s = lax.dot_general(
-                    jnp.concatenate([k, k], axis=1), q, BOTH, preferred_element_type=jnp.float32
+                    k, q, BOTH, preferred_element_type=jnp.float32
                 )
                 s_new[c : c + TILE, :] = s
                 top = jnp.max(s.reshape(TILE // 8, 8, rows), axis=0)
                 best = top if best is None else jnp.maximum(best, top)
             if used is not None:
-                p = jnp.exp2(s_old[c : c + TILE, :] - m)
-                t = jnp.sum(p.reshape(TILE // 8, 8, rows), axis=0)
+                p = jnp.exp2(s_old[c : c + TILE, :] * scale - m)
                 d = jnp.dot(
                     v_all[now_k, :, c : c + TILE],
                     p.astype(jnp.bfloat16),
                     preferred_element_type=jnp.float32,
                 )
-                sums = t if sums is None else sums + t
                 acc = d if acc is None else acc + d
         if used is not None:
-            total[now_q] = total[now_q] * f + sums
-            mixed[now_q] = mixed[now_q] * f + acc
+            total[now_q] = total[now_q] * f + acc[size : size + 8]
+            mixed[now_q] = mixed[now_q] * f + acc[:size]
         if fresh is not None:
             before = run_max[next_q]
             after = jnp.maximum(before, jnp.max(best, axis=0, keepdims=True))
             run_max[next_q] = after
-            m_new[...] = after
-            f_new[...] = jnp.exp2(before - after)
+            m_new[...] = after * scale
+            f_new[...] = jnp.exp2((before - after) * scale)
 
     return step
 
@@ -157,14 +153,15 @@
     place, order, mask, own, run_max, total, mixed, v_all, q_all, k_all, *bufs, toks, share
 ):
     core = place[0]
-    groups = own.shape[0] // 2
+    groups, size = own.shape[0] // 2, own.shape[-1]
     clear(run_max, total, mixed)
     load_own(own, core, toks, share, q_all, k_all)
     step = make_step(q_all, k_all, v_all, (run_max, total, mixed), groups * toks)
     a, b = bufs[0::2], bufs[1::2]
+    v_all[:, size:] = jnp.ones((2, 16, groups * toks), jnp.bfloat16)
     step((0, 0), a, None, None)
     for slot in range(2):
-        v_all[slot] = turn(own[slot * groups : (slot + 1) * groups, toks : 2 * toks, :])
+        v_all[slot, :size] = turn(own[slot * groups : (slot + 1) * groups, toks : 2 * toks, :])
     step((1, 1), b, (0, 0), a)
     here, there = order[stretch_of(0, core)], order[stretch_of(1, core)]
     later = jnp.where(here > there, 0, 1)
@@ -226,15 +223,16 @@
     def pair(n):
         return pair_q[n], pair_k[n]
 
+    for copy in copies[0:2]:
+        copy.wait()
+    load_queries(q_raw[0], 2, q_all)
+    v_all[2:4, size:] = jnp.ones((2, 16, groups * toks), jnp.bfloat16)
+    step((2, 2), a, None, None)
+    for copy in copies[2:]:
+        copy.wait()
+    load_queries(q_raw[1], 3, q_all)
     for slot in range(2):
-        copies[3 * slot].wait()
-        copies[3 * slot + 1].wait()
-        load_queries(q_raw[slot], 2 + slot, q_all)
-    for slot in range(2):
-        copies[3 * slot + 2].wait()
-    step((2, 2), a, None, None)
-    for slot in range(2):
-        v_all[2 + slot] = turn(v_raw[slot])
+        v_all[2 + slot, :size] = turn(v_raw[slot])
 
     steps = count - 1
 
@@ -255,7 +253,7 @@
     for slot in range(4):
         stretch = stretch_of(slot, core)
         gate = gates[levels[stretch], pl.ds(head, 1), :]
-        o = mixed[slot] / jnp.sum(total[slot], axis=0, keepdims=True)
+        o = mixed[slot] / total[slot, 0:1, :]
         out[stretch] = (o.T * gate).astype(jnp.bfloat16).reshape(groups, share, size)
 
 
@@ -266,7 +264,7 @@
 def scratch(n, groups, toks, share, size):
     f32, bf16 = jnp.float32, jnp.bfloat16
     rows, keys = groups * share, groups * toks
-    head = [pltpu.VMEM((n, rows, 2 * size), bf16), pltpu.VMEM((n, groups, toks, size), bf16)]
+    head = [pltpu.VMEM((n, rows, size), bf16), pltpu.VMEM((n, groups, toks, size), bf16)]
     bufs = [pltpu.VMEM((keys, rows), f32)] * 2 + [pltpu.VMEM((8, rows), f32)] * 4
     return head, bufs
 
@@ -276,7 +274,7 @@
     rows, keys = groups * share, groups * toks
     head, bufs = scratch(2, groups, toks, share, size)
     shapes = [jax.ShapeDtypeStruct(s, jnp.float32) for s in state_of(2, rows, size)]
-    shapes.append(jax.ShapeDtypeStruct((2, size, keys), jnp.bfloat16))
+    shapes.append(jax.ShapeDtypeStruct((2, size + 16, keys), jnp.bfloat16))
     return pl.pallas_call(
         functools.partial(first_kernel, toks=toks, share=share),
         out_shape=shapes,
@@ -303,7 +301,7 @@
         pltpu.VMEM((2, groups, share, size), jnp.bfloat16),
         pltpu.VMEM((2, groups, toks, size), jnp.bfloat16),
     ]
-    mine = [pltpu.VMEM((4, size, keys), jnp.bfloat16)]
+    mine = [pltpu.VMEM((4, size + 16, keys), jnp.bfloat16)]
     mine += [pltpu.VMEM(s, jnp.float32) for s in state_of(4, rows, size)]
     return pl.pallas_call(
         functools.partial(rest_kernel, toks=toks, share=share),

time: 85.3 us -> 84.6 us (level)
  Pallas kernels: 17.6 us -> 15.7 us
  blocking collectives: 63.3 us -> 64.5 us
    pallas_call x1, Pallas kernels: 10.2 us -> 8.46 us  [rest(): pl.pallas_call(functools.partial(rest_kernel, toks=toks, share=share), ou...]
    all_to_all x1, blocking collectives: 17.3 us -> 18.4 us  [shards(): lax.all_to_all(part.reshape(4 * heads, share, size), ('xh', 'core', 'ctx'...]
  transfers between devices with their start and end apart: 1 -> 1, of which waited for: 0 -> 1; matrix products, arithmetic and copies ran while one was open for 0% -> 0% of each run, Pallas kernels for 5% -> 5%
where the time goes in v5:
time: 84.6 us; the launch traced here: 83.8 us
  blocking collectives  64.5 us (76%)
  Pallas kernels  15.7 us (19%)
  starting transfers between devices  2.46 us (3%)
  local copies, waits for them, and re-layouts  0.95 us (1%)
    all_to_all x1, blocking collectives, shards(): lax.all_to_all(pack(queries[0], keys[0], values[0]), ('xh', 'ctx'), 0, 0,...  46 us
    all_to_all x1, blocking collectives, shards(): lax.all_to_all(part.reshape(4 * heads, share, size), ('xh', 'core', 'ctx'...  18.4 us
    pallas_call x1, Pallas kernels, rest(): pl.pallas_call(functools.partial(rest_kernel, toks=toks, share=share), ou...  8.46 us
    pallas_call x1, Pallas kernels, first(): pl.pallas_call(functools.partial(first_kernel, toks=toks, share=share), o...  4.47 us
    pallas_call x1, Pallas kernels, pack(): pl.pallas_call(pack_kernel, out_shape=jax.ShapeDtypeStruct((2 * heads, 2...  2.73 us
    ppermute x1, starting transfers between devices, shards(): other = lax.ppermute(own, 'core', SWAP)  2.46 us
  transfers between devices with their start and end apart: 1, of which 1 were waited for; matrix products, arithmetic and copies ran while one was open for 0% of the time, Pallas kernels for 5%

profile of v5, /device:TPU:1, one launch (start us, length us, event | category | flops | bytes accessed | tf_op | source)
XLA Modules:
  0.0 83.8 jit_solution(11588845145932436299)
XLA Ops:
  0.0 2.7 %shard_map.73 = bf16[64,160,128]{2,1,0:T(8,128)(2,1)} custom-call(bf16[64,32,128]{2,1,0:T(8,128)(2,1)} %bitcast.12, bf16[64,32,128]{2,1,0:T(8,128)(2,1)} %bitcast.13, bf16[64,32,128]{2,1,0:T(8,128)(2,1)} %bitcast.14), custom_call_target="tpu_custom_call" | custom-call | tf_op jit(solution)/shard_map/pallas_call | solution.py:57
  2.7 0.0 copy-start.1
  2.7 0.0 copy-start.2
  2.8 46.0 %all_to_all.10.own = bf16[64,160,128]{2,1,0:T(8,128)(2,1)S(1)} all-to-all(bf16[64,160,128]{2,1,0:T(8,128)(2,1)} %shard_map.73), channel_id=1, replica_groups=mesh['xh'=2,'core'=2,'ctx'=32] {'xh','ctx'}, dimensions={0} | all-to-all | bytes 5242880 | tf_op jit(solution)/shard_map/all_to_all | solution.py:319
  48.8 2.5 %collective-permute-start = (bf16[64,160,128]{2,1,0:T(8,128)(2,1)S(1)}, bf16[64,160,128]{2,1,0:T(8,128)(2,1)}, u32[]{:S(2)}, u32[]{:S(2)}) collective-permute-start(bf16[64,160,128]{2,1,0:T(8,128)(2,1)S(1)} %all_to_all.10.own), channel_id=1, source_target_pairs={{0,32},{32,0},{1,33},{33,1},{2,34},{34,2},{3,35},{35,3},{4,36},{36... | collective-permute-start | bytes 7864328 | tf_op jit(solution)/shard_map/ppermute | solution.py:320
  51.3 0.1 pad_add_fusion.place
  51.3 0.0 copy-done.1
  51.3 0.0 copy-done.2
  51.3 0.0 copy-start
  51.3 0.0 copy-start.3
  51.3 4.5 %shard_map.74 = (f32[2,8,512]{2,1,0:T(8,128)S(1)}, f32[2,8,512]{2,1,0:T(8,128)S(1)}, f32[2,128,512]{2,1,0:T(8,128)S(1)}, bf16[2,144,2048]{2,1,0:T(8,128)(2,1)S(1)}) custom-call(s32[2]{0:T(128)S(1)} %pad_add_fusion.place, s32[4]{0:T(128)S(1)} %copy-done.2, s32[4,4]{1,0:T(4,128)S(1)} %copy-done.1, bf16[64,160,128]{2,1,0:T(8,128)(2,1)S(1)} %all_to_all.10.own), custom_call_target="tpu_custom_call" | custom-call | flops 1610612736 | bytes 8388608 | tf_op jit(solution)/shard_map/pallas_call | solution.py:278
  55.8 0.1 collective-permute-done.other
  55.9 0.0 copy-done
  55.9 0.0 copy-done.3
  55.9 8.5 %shard_map.75 = bf16[4,32,16,128]{3,2,1,0:T(8,128)(2,1)S(1)} custom-call(s32[2]{0:T(128)S(1)} %pad_add_fusion.place, s32[4]{0:T(128)S(1)} %copy-done.2, s32[4]{0:T(128)S(1)} %copy-done.3, s32[4,4]{1,0:T(4,128)S(1)} %copy-done.1, bf16[64,160,128]{2,1,0:T(8,128)(2,1)S(1)} %all_to_all.10.own, bf16[64,160,128]{2,1,0:T(8,128)(2,1)} %collective-permute-done.other, ...), custom_call_target="tpu_custom_call" | custom-call | tf_op jit(solution)/shard_map/pallas_call | solution.py:306
  64.4 18.4 %all_to_all.11 = bf16[128,16,128]{2,1,0:T(8,128)(2,1)S(1)} all-to-all(bf16[128,16,128]{2,1,0:T(8,128)(2,1)S(1)} %bitcast.10), channel_id=1, replica_groups=mesh['xh'=2,'core'=2,'ctx'=32] {'xh','core','ctx'}, dimensions={0} | all-to-all | bytes 1048576 | tf_op jit(solution)/shard_map/all_to_all | solution.py:326
  82.8 0.9 %copy.8 = bf16[4,32,16,128]{3,1,2,0:T(8,128)(2,1)} copy(bf16[4,32,16,128]{3,2,1,0:T(8,128)(2,1)S(1)} %bitcast.11) | data formatting | bytes 1048576 | tf_op jit(solution)/shard_map/reshape | solution.py:329
Async XLA Ops:
  2.7 48.6 %copy-start.1 = (s32[4,4]{1,0:T(4,128)S(1)}, s32[4,4]{1,0:T(4,128)}, u32[]{:S(2)}) copy-start(s32[4,4]{1,0:T(4,128)} %mask.3) | copy-start | bytes 196
  2.7 48.6 %copy-start.2 = (s32[4]{0:T(128)S(1)}, s32[4]{0:T(128)}, u32[]{:S(2)}) copy-start(s32[4]{0:T(128)} %order.3) | copy-start | bytes 52
  48.8 7.1 %collective-permute-start = (bf16[64,160,128]{2,1,0:T(8,128)(2,1)S(1)}, bf16[64,160,128]{2,1,0:T(8,128)(2,1)}, u32[]{:S(2)}, u32[]{:S(2)}) collective-permute-start(bf16[64,160,128]{2,1,0:T(8,128)(2,1)S(1)} %all_to_all.10.own), channel_id=1, source_target_pairs={{0,32},{32,0},{1,33},{33,1},{2,34},{34,2},{3,35},{35,3},{4,36},{36... | collective-permute-start | bytes 7864328 | tf_op jit(solution)/shard_map/ppermute | solution.py:320
  51.3 4.6 %copy-start = (f32[8,32,128]{2,1,0:T(8,128)S(1)}, f32[8,32,128]{2,1,0:T(8,128)}, u32[]{:S(2)}) copy-start(f32[8,32,128]{2,1,0:T(8,128)} %gates.1) | copy-start | bytes 393220
  51.3 4.6 %copy-start.3 = (s32[4]{0:T(128)S(1)}, s32[4]{0:T(128)}, u32[]{:S(2)}) copy-start(s32[4]{0:T(128)} %levels.1) | copy-start | bytes 52

commit v6 on v5

--- a/solution.py
+++ b/solution.py
@@ -11,6 +11,7 @@
 SWAP = [(0, 1), (1, 0)]
 BOTH = (((1,), (1,)), ((), ()))
 TILE = 512
+MIX_TILE = 256
 SMEM = pl.BlockSpec(memory_space=pltpu.SMEM)
 VMEM = pl.BlockSpec(memory_space=pltpu.VMEM)
 LIMIT = 48 * 2**20
@@ -113,23 +114,22 @@
             s_new, m_new, f_new = new
             next_q, next_k = fresh
             q = q_all[next_q]
-        for c in range(0, keys, TILE):
+        for base in range(0, keys, TILE):
             if fresh is not None:
-                k = k_all[next_k, c // toks : (c + TILE) // toks].reshape(TILE, size)
-                s = lax.dot_general(
-                    k, q, BOTH, preferred_element_type=jnp.float32
-                )
-                s_new[c : c + TILE, :] = s
+                k = k_all[next_k, base // toks : (base + TILE) // toks].reshape(TILE, size)
+                s = lax.dot_general(k, q, BOTH, preferred_element_type=jnp.float32)
+                s_new[base : base + TILE, :] = s
                 top = jnp.max(s.reshape(TILE // 8, 8, rows), axis=0)
                 best = top if best is None else jnp.maximum(best, top)
             if used is not None:
-                p = jnp.exp2(s_old[c : c + TILE, :] * scale - m)
-                d = jnp.dot(
-                    v_all[now_k, :, c : c + TILE],
-                    p.astype(jnp.bfloat16),
-                    preferred_element_type=jnp.float32,
-                )
-                acc = d if acc is None else acc + d
+                for c in range(base, base + TILE, MIX_TILE):
+                    p = jnp.exp2(s_old[c : c + MIX_TILE, :] * scale - m)
+                    d = jnp.dot(
+                        v_all[now_k, :, c : c + MIX_TILE],
+                        p.astype(jnp.bfloat16),
+                        preferred_element_type=jnp.float32,
+                    )
+                    acc = d if acc is None else acc + d
         if used is not None:
             total[now_q] = total[now_q] * f + acc[size : size + 8]
             mixed[now_q] = mixed[now_q] * f + acc[:size]

time: 84.6 us -> 84.1 us (level); the launches traced: 83.8 us -> 84.5 us
  no operation moved by 1% of the time
where the time goes in v6:
time: 84.1 us; the launch traced here: 84.5 us
  blocking collectives  64.5 us (77%)
  Pallas kernels  16.5 us (20%)
  starting transfers between devices  2.46 us (3%)
  local copies, waits for them, and re-layouts  0.95 us (1%)
    all_to_all x1, blocking collectives, shards(): lax.all_to_all(pack(queries[0], keys[0], values[0]), ('xh', 'ctx'), 0, 0,...  46 us
    all_to_all x1, blocking collectives, shards(): lax.all_to_all(part.reshape(4 * heads, share, size), ('xh', 'core', 'ctx'...  18.4 us
    pallas_call x1, Pallas kernels, rest(): pl.pallas_call(functools.partial(rest_kernel, toks=toks, share=share), ou...  9.24 us
    pallas_call x1, Pallas kernels, first(): pl.pallas_call(functools.partial(first_kernel, toks=toks, share=share), o...  4.52 us
    pallas_call x1, Pallas kernels, pack(): pl.pallas_call(pack_kernel, out_shape=jax.ShapeDtypeStruct((2 * heads, 2...  2.73 us
    ppermute x1, starting transfers between devices, shards(): other = lax.ppermute(own, 'core', SWAP)  2.46 us
  transfers between devices with their start and end apart: 1, of which 1 were waited for; matrix products, arithmetic and copies ran while one was open for 0% of the time, Pallas kernels for 5%

profile of v6, /device:TPU:1, one launch (start us, length us, event | category | flops | bytes accessed | tf_op | source)
XLA Modules:
  0.0 84.5 jit_solution(6339718252554057348)
XLA Ops:
  0.0 2.7 %shard_map.73 = bf16[64,160,128]{2,1,0:T(8,128)(2,1)} custom-call(bf16[64,32,128]{2,1,0:T(8,128)(2,1)} %bitcast.12, bf16[64,32,128]{2,1,0:T(8,128)(2,1)} %bitcast.13, bf16[64,32,128]{2,1,0:T(8,128)(2,1)} %bitcast.14), custom_call_target="tpu_custom_call" | custom-call | tf_op jit(solution)/shard_map/pallas_call | solution.py:58
  2.7 0.0 copy-start.1
  2.7 0.0 copy-start.2
  2.8 46.0 %all_to_all.10.own = bf16[64,160,128]{2,1,0:T(8,128)(2,1)S(1)} all-to-all(bf16[64,160,128]{2,1,0:T(8,128)(2,1)} %shard_map.73), channel_id=1, replica_groups=mesh['xh'=2,'core'=2,'ctx'=32] {'xh','ctx'}, dimensions={0} | all-to-all | bytes 5242880 | tf_op jit(solution)/shard_map/all_to_all | solution.py:319
  48.8 2.5 %collective-permute-start = (bf16[64,160,128]{2,1,0:T(8,128)(2,1)S(1)}, bf16[64,160,128]{2,1,0:T(8,128)(2,1)}, u32[]{:S(2)}, u32[]{:S(2)}) collective-permute-start(bf16[64,160,128]{2,1,0:T(8,128)(2,1)S(1)} %all_to_all.10.own), channel_id=1, source_target_pairs={{0,32},{32,0},{1,33},{33,1},{2,34},{34,2},{3,35},{35,3},{4,36},{36... | collective-permute-start | bytes 7864328 | tf_op jit(solution)/shard_map/ppermute | solution.py:320
  51.3 0.1 pad_add_fusion.place
  51.3 0.0 copy-done.1
  51.3 0.0 copy-done.2
  51.3 0.0 copy-start
  51.3 0.0 copy-start.3
  51.3 4.5 %shard_map.74 = (f32[2,8,512]{2,1,0:T(8,128)S(1)}, f32[2,8,512]{2,1,0:T(8,128)S(1)}, f32[2,128,512]{2,1,0:T(8,128)S(1)}, bf16[2,144,2048]{2,1,0:T(8,128)(2,1)S(1)}) custom-call(s32[2]{0:T(128)S(1)} %pad_add_fusion.place, s32[4]{0:T(128)S(1)} %copy-done.2, s32[4,4]{1,0:T(4,128)S(1)} %copy-done.1, bf16[64,160,128]{2,1,0:T(8,128)(2,1)S(1)} %all_to_all.10.own), custom_call_target="tpu_custom_call" | custom-call | flops 1610612736 | bytes 8388608 | tf_op jit(solution)/shard_map/pallas_call | solution.py:278
  55.9 0.1 collective-permute-done.other
  55.9 0.0 copy-done
  55.9 0.0 copy-done.3
  55.9 9.2 %shard_map.75 = bf16[4,32,16,128]{3,2,1,0:T(8,128)(2,1)S(1)} custom-call(s32[2]{0:T(128)S(1)} %pad_add_fusion.place, s32[4]{0:T(128)S(1)} %copy-done.2, s32[4]{0:T(128)S(1)} %copy-done.3, s32[4,4]{1,0:T(4,128)S(1)} %copy-done.1, bf16[64,160,128]{2,1,0:T(8,128)(2,1)S(1)} %all_to_all.10.own, bf16[64,160,128]{2,1,0:T(8,128)(2,1)} %collective-permute-done.other, ...), custom_call_target="tpu_custom_call" | custom-call | tf_op jit(solution)/shard_map/pallas_call | solution.py:306
  65.2 18.4 %all_to_all.11 = bf16[128,16,128]{2,1,0:T(8,128)(2,1)S(1)} all-to-all(bf16[128,16,128]{2,1,0:T(8,128)(2,1)S(1)} %bitcast.10), channel_id=1, replica_groups=mesh['xh'=2,'core'=2,'ctx'=32] {'xh','core','ctx'}, dimensions={0} | all-to-all | bytes 1048576 | tf_op jit(solution)/shard_map/all_to_all | solution.py:326
  83.6 0.9 %copy.8 = bf16[4,32,16,128]{3,1,2,0:T(8,128)(2,1)} copy(bf16[4,32,16,128]{3,2,1,0:T(8,128)(2,1)S(1)} %bitcast.11) | data formatting | bytes 1048576 | tf_op jit(solution)/shard_map/reshape | solution.py:329
Async XLA Ops:
  2.7 48.6 %copy-start.1 = (s32[4,4]{1,0:T(4,128)S(1)}, s32[4,4]{1,0:T(4,128)}, u32[]{:S(2)}) copy-start(s32[4,4]{1,0:T(4,128)} %mask.3) | copy-start | bytes 196
  2.7 48.6 %copy-start.2 = (s32[4]{0:T(128)S(1)}, s32[4]{0:T(128)}, u32[]{:S(2)}) copy-start(s32[4]{0:T(128)} %order.3) | copy-start | bytes 52
  48.8 7.1 %collective-permute-start = (bf16[64,160,128]{2,1,0:T(8,128)(2,1)S(1)}, bf16[64,160,128]{2,1,0:T(8,128)(2,1)}, u32[]{:S(2)}, u32[]{:S(2)}) collective-permute-start(bf16[64,160,128]{2,1,0:T(8,128)(2,1)S(1)} %all_to_all.10.own), channel_id=1, source_target_pairs={{0,32},{32,0},{1,33},{33,1},{2,34},{34,2},{3,35},{35,3},{4,36},{36... | collective-permute-start | bytes 7864328 | tf_op jit(solution)/shard_map/ppermute | solution.py:320
  51.3 4.6 %copy-start = (f32[8,32,128]{2,1,0:T(8,128)S(1)}, f32[8,32,128]{2,1,0:T(8,128)}, u32[]{:S(2)}) copy-start(f32[8,32,128]{2,1,0:T(8,128)} %gates.1) | copy-start | bytes 393220
  51.3 4.6 %copy-start.3 = (s32[4]{0:T(128)S(1)}, s32[4]{0:T(128)}, u32[]{:S(2)}) copy-start(s32[4]{0:T(128)} %levels.1) | copy-start | bytes 52

commit v7 on v6

--- a/solution.py
+++ b/solution.py
@@ -196,11 +196,13 @@
             copy = pltpu.make_async_copy(other.at[at, rows], dst, sems.at[len(copies)])
             copy.start()
             copies.append(copy)
+    copy = pltpu.make_async_copy(v_in, v_all.at[pl.ds(0, 2)], sems.at[len(copies)])
+    copy.start()
+    copies.append(copy)
     clear(run_max.at[2:4], total.at[2:4], mixed.at[2:4])
     run_max[0:2] = max_in[...]
     total[0:2] = total_in[...]
     mixed[0:2] = mixed_in[...]
-    v_all[0:2] = v_in[...]
     load_own(own, core, toks, share, q_all, k_all)
 
     count = jnp.int32(0)
@@ -297,7 +299,7 @@
     lists = [
         pltpu.SMEM((17,), jnp.int32),
         pltpu.SMEM((17,), jnp.int32),
-        pltpu.SemaphoreType.DMA((6,)),
+        pltpu.SemaphoreType.DMA((7,)),
         pltpu.VMEM((2, groups, share, size), jnp.bfloat16),
         pltpu.VMEM((2, groups, toks, size), jnp.bfloat16),
     ]

time: 84.1 us -> 84.3 us (level)
  Pallas kernels: 16.5 us -> 17.6 us
  blocking collectives: 64.5 us -> 63.4 us
    pallas_call x1, Pallas kernels: 9.24 us -> 10.4 us  [rest(): pl.pallas_call(functools.partial(rest_kernel, toks=toks, share=share), ou...]
    all_to_all x1, blocking collectives: 18.4 us -> 17.3 us  [shards(): lax.all_to_all(part.reshape(4 * heads, share, size), ('xh', 'core', 'ctx'...]
where the time goes in v7:
time: 84.3 us; the launch traced here: 84.6 us
  blocking collectives  63.4 us (75%)
  Pallas kernels  17.6 us (21%)
  starting transfers between devices  2.46 us (3%)
  local copies, waits for them, and re-layouts  0.95 us (1%)
    all_to_all x1, blocking collectives, shards(): lax.all_to_all(pack(queries[0], keys[0], values[0]), ('xh', 'ctx'), 0, 0,...  46 us
    all_to_all x1, blocking collectives, shards(): lax.all_to_all(part.reshape(4 * heads, share, size), ('xh', 'core', 'ctx'...  17.3 us
    pallas_call x1, Pallas kernels, rest(): pl.pallas_call(functools.partial(rest_kernel, toks=toks, share=share), ou...  10.4 us
    pallas_call x1, Pallas kernels, first(): pl.pallas_call(functools.partial(first_kernel, toks=toks, share=share), o...  4.52 us
    pallas_call x1, Pallas kernels, pack(): pl.pallas_call(pack_kernel, out_shape=jax.ShapeDtypeStruct((2 * heads, 2...  2.73 us
    ppermute x1, starting transfers between devices, shards(): other = lax.ppermute(own, 'core', SWAP)  2.46 us
  transfers between devices with their start and end apart: 1, of which 1 were waited for; matrix products, arithmetic and copies ran while one was open for 0% of the time, Pallas kernels for 5%

profile of v7, /device:TPU:1, one launch (start us, length us, event | category | flops | bytes accessed | tf_op | source)
XLA Modules:
  0.0 84.6 jit_solution(16901472845336814774)
XLA Ops:
  0.0 2.7 %shard_map.73 = bf16[64,160,128]{2,1,0:T(8,128)(2,1)} custom-call(bf16[64,32,128]{2,1,0:T(8,128)(2,1)} %bitcast.12, bf16[64,32,128]{2,1,0:T(8,128)(2,1)} %bitcast.13, bf16[64,32,128]{2,1,0:T(8,128)(2,1)} %bitcast.14), custom_call_target="tpu_custom_call" | custom-call | tf_op jit(solution)/shard_map/pallas_call | solution.py:58
  2.7 0.0 copy-start.1
  2.7 0.0 copy-start.2
  2.8 46.0 %all_to_all.10.own = bf16[64,160,128]{2,1,0:T(8,128)(2,1)S(1)} all-to-all(bf16[64,160,128]{2,1,0:T(8,128)(2,1)} %shard_map.73), channel_id=1, replica_groups=mesh['xh'=2,'core'=2,'ctx'=32] {'xh','ctx'}, dimensions={0} | all-to-all | bytes 5242880 | tf_op jit(solution)/shard_map/all_to_all | solution.py:321
  48.8 2.5 %collective-permute-start = (bf16[64,160,128]{2,1,0:T(8,128)(2,1)S(1)}, bf16[64,160,128]{2,1,0:T(8,128)(2,1)}, u32[]{:S(2)}, u32[]{:S(2)}) collective-permute-start(bf16[64,160,128]{2,1,0:T(8,128)(2,1)S(1)} %all_to_all.10.own), channel_id=1, source_target_pairs={{0,32},{32,0},{1,33},{33,1},{2,34},{34,2},{3,35},{35,3},{4,36},{36... | collective-permute-start | bytes 7864328 | tf_op jit(solution)/shard_map/ppermute | solution.py:322
  51.3 0.1 pad_add_fusion.place
  51.3 0.0 copy-done.1
  51.3 0.0 copy-done.2
  51.3 0.0 copy-start
  51.3 0.0 copy-start.3
  51.3 4.5 %shard_map.74 = (f32[2,8,512]{2,1,0:T(8,128)S(1)}, f32[2,8,512]{2,1,0:T(8,128)S(1)}, f32[2,128,512]{2,1,0:T(8,128)S(1)}, bf16[2,144,2048]{2,1,0:T(8,128)(2,1)S(1)}) custom-call(s32[2]{0:T(128)S(1)} %pad_add_fusion.place, s32[4]{0:T(128)S(1)} %copy-done.2, s32[4,4]{1,0:T(4,128)S(1)} %copy-done.1, bf16[64,160,128]{2,1,0:T(8,128)(2,1)S(1)} %all_to_all.10.own), custom_call_target="tpu_custom_call" | custom-call | flops 1610612736 | bytes 8388608 | tf_op jit(solution)/shard_map/pallas_call | solution.py:280
  55.9 0.1 collective-permute-done.other
  55.9 0.0 copy-done
  55.9 0.0 copy-done.3
  55.9 10.4 %shard_map.75 = bf16[4,32,16,128]{3,2,1,0:T(8,128)(2,1)S(1)} custom-call(s32[2]{0:T(128)S(1)} %pad_add_fusion.place, s32[4]{0:T(128)S(1)} %copy-done.2, s32[4]{0:T(128)S(1)} %copy-done.3, s32[4,4]{1,0:T(4,128)S(1)} %copy-done.1, bf16[64,160,128]{2,1,0:T(8,128)(2,1)S(1)} %all_to_all.10.own, bf16[64,160,128]{2,1,0:T(8,128)(2,1)} %collective-permute-done.other, ...), custom_call_target="tpu_custom_call" | custom-call | tf_op jit(solution)/shard_map/pallas_call | solution.py:308
  66.3 17.3 %all_to_all.11 = bf16[128,16,128]{2,1,0:T(8,128)(2,1)S(1)} all-to-all(bf16[128,16,128]{2,1,0:T(8,128)(2,1)S(1)} %bitcast.10), channel_id=1, replica_groups=mesh['xh'=2,'core'=2,'ctx'=32] {'xh','core','ctx'}, dimensions={0} | all-to-all | bytes 1048576 | tf_op jit(solution)/shard_map/all_to_all | solution.py:328
  83.6 0.9 %copy.8 = bf16[4,32,16,128]{3,1,2,0:T(8,128)(2,1)} copy(bf16[4,32,16,128]{3,2,1,0:T(8,128)(2,1)S(1)} %bitcast.11) | data formatting | bytes 1048576 | tf_op jit(solution)/shard_map/reshape | solution.py:331
Async XLA Ops:
  2.7 48.6 %copy-start.1 = (s32[4,4]{1,0:T(4,128)S(1)}, s32[4,4]{1,0:T(4,128)}, u32[]{:S(2)}) copy-start(s32[4,4]{1,0:T(4,128)} %mask.3) | copy-start | bytes 196
  2.7 48.6 %copy-start.2 = (s32[4]{0:T(128)S(1)}, s32[4]{0:T(128)}, u32[]{:S(2)}) copy-start(s32[4]{0:T(128)} %order.3) | copy-start | bytes 52
  48.8 7.1 %collective-permute-start = (bf16[64,160,128]{2,1,0:T(8,128)(2,1)S(1)}, bf16[64,160,128]{2,1,0:T(8,128)(2,1)}, u32[]{:S(2)}, u32[]{:S(2)}) collective-permute-start(bf16[64,160,128]{2,1,0:T(8,128)(2,1)S(1)} %all_to_all.10.own), channel_id=1, source_target_pairs={{0,32},{32,0},{1,33},{33,1},{2,34},{34,2},{3,35},{35,3},{4,36},{36... | collective-permute-start | bytes 7864328 | tf_op jit(solution)/shard_map/ppermute | solution.py:322
  51.3 4.6 %copy-start = (f32[8,32,128]{2,1,0:T(8,128)S(1)}, f32[8,32,128]{2,1,0:T(8,128)}, u32[]{:S(2)}) copy-start(f32[8,32,128]{2,1,0:T(8,128)} %gates.1) | copy-start | bytes 393220
  51.3 4.6 %copy-start.3 = (s32[4]{0:T(128)S(1)}, s32[4]{0:T(128)}, u32[]{:S(2)}) copy-start(s32[4]{0:T(128)} %levels.1) | copy-start | bytes 52

commit v8 on v6

--- a/solution.py
+++ b/solution.py
@@ -196,11 +196,13 @@
             copy = pltpu.make_async_copy(other.at[at, rows], dst, sems.at[len(copies)])
             copy.start()
             copies.append(copy)
+    for src, dst in ((v_in, v_all), (mixed_in, mixed)):
+        copy = pltpu.make_async_copy(src, dst.at[pl.ds(0, 2)], sems.at[len(copies)])
+        copy.start()
+        copies.append(copy)
     clear(run_max.at[2:4], total.at[2:4], mixed.at[2:4])
     run_max[0:2] = max_in[...]
     total[0:2] = total_in[...]
-    mixed[0:2] = mixed_in[...]
-    v_all[0:2] = v_in[...]
     load_own(own, core, toks, share, q_all, k_all)
 
     count = jnp.int32(0)
@@ -297,7 +299,7 @@
     lists = [
         pltpu.SMEM((17,), jnp.int32),
         pltpu.SMEM((17,), jnp.int32),
-        pltpu.SemaphoreType.DMA((6,)),
+        pltpu.SemaphoreType.DMA((8,)),
         pltpu.VMEM((2, groups, share, size), jnp.bfloat16),
         pltpu.VMEM((2, groups, toks, size), jnp.bfloat16),
     ]

time: 84.1 us -> 83.7 us (level)
  blocking collectives: 64.5 us -> 63.1 us
  waiting for transfers between devices: 0.06 us -> 1.1 us
    all_to_all x1, blocking collectives: 18.4 us -> 17.1 us  [shards(): lax.all_to_all(part.reshape(4 * heads, share, size), ('xh', 'core', 'ctx'...]
    pallas_call x1, Pallas kernels: 9.24 us -> 10.4 us  [rest(): pl.pallas_call(functools.partial(rest_kernel, toks=toks, share=share), ou...]
    ppermute x1, waiting for transfers between devices: 0.06 us -> 1.1 us  [shards(): other = lax.ppermute(own, 'core', SWAP)]
    pallas_call x1, Pallas kernels: 4.52 us -> 3.48 us  [first(): pl.pallas_call(functools.partial(first_kernel, toks=toks, share=share), o...]
  transfers between devices with their start and end apart: 1 -> 1, of which waited for: 1 -> 1; matrix products, arithmetic and copies ran while one was open for 0% -> 0% of each run, Pallas kernels for 5% -> 4%
where the time goes in v8:
time: 83.7 us; the launch traced here: 84.3 us
  blocking collectives  63.1 us (75%)
  Pallas kernels  16.6 us (20%)
  starting transfers between devices  2.46 us (3%)
  waiting for transfers between devices  1.1 us (1%)
  local copies, waits for them, and re-layouts  0.95 us (1%)
    all_to_all x1, blocking collectives, shards(): lax.all_to_all(pack(queries[0], keys[0], values[0]), ('xh', 'ctx'), 0, 0,...  46 us
    all_to_all x1, blocking collectives, shards(): lax.all_to_all(part.reshape(4 * heads, share, size), ('xh', 'core', 'ctx'...  17.1 us
    pallas_call x1, Pallas kernels, rest(): pl.pallas_call(functools.partial(rest_kernel, toks=toks, share=share), ou...  10.4 us
    pallas_call x1, Pallas kernels, first(): pl.pallas_call(functools.partial(first_kernel, toks=toks, share=share), o...  3.48 us
    pallas_call x1, Pallas kernels, pack(): pl.pallas_call(pack_kernel, out_shape=jax.ShapeDtypeStruct((2 * heads, 2...  2.73 us
    ppermute x1, starting transfers between devices, shards(): other = lax.ppermute(own, 'core', SWAP)  2.46 us
  transfers between devices with their start and end apart: 1, of which 1 were waited for; matrix products, arithmetic and copies ran while one was open for 0% of the time, Pallas kernels for 4%

profile of v8, /device:TPU:1, one launch (start us, length us, event | category | flops | bytes accessed | tf_op | source)
XLA Modules:
  0.0 84.3 jit_solution(14482793548765972889)
XLA Ops:
  0.0 2.7 %shard_map.73 = bf16[64,160,128]{2,1,0:T(8,128)(2,1)} custom-call(bf16[64,32,128]{2,1,0:T(8,128)(2,1)} %bitcast.12, bf16[64,32,128]{2,1,0:T(8,128)(2,1)} %bitcast.13, bf16[64,32,128]{2,1,0:T(8,128)(2,1)} %bitcast.14), custom_call_target="tpu_custom_call" | custom-call | tf_op jit(solution)/shard_map/pallas_call | solution.py:58
  2.7 0.0 copy-start.1
  2.7 0.0 copy-start.2
  2.8 46.0 %all_to_all.10.own = bf16[64,160,128]{2,1,0:T(8,128)(2,1)S(1)} all-to-all(bf16[64,160,128]{2,1,0:T(8,128)(2,1)} %shard_map.73), channel_id=1, replica_groups=mesh['xh'=2,'core'=2,'ctx'=32] {'xh','ctx'}, dimensions={0} | all-to-all | bytes 5242880 | tf_op jit(solution)/shard_map/all_to_all | solution.py:321
  48.8 2.5 %collective-permute-start = (bf16[64,160,128]{2,1,0:T(8,128)(2,1)S(1)}, bf16[64,160,128]{2,1,0:T(8,128)(2,1)}, u32[]{:S(2)}, u32[]{:S(2)}) collective-permute-start(bf16[64,160,128]{2,1,0:T(8,128)(2,1)S(1)} %all_to_all.10.own), channel_id=1, source_target_pairs={{0,32},{32,0},{1,33},{33,1},{2,34},{34,2},{3,35},{35,3},{4,36},{36... | collective-permute-start | bytes 7864328 | tf_op jit(solution)/shard_map/ppermute | solution.py:322
  51.3 0.1 pad_add_fusion.place
  51.3 0.0 copy-done.1
  51.3 0.0 copy-done.2
  51.3 0.0 copy-start
  51.3 0.0 copy-start.3
  51.3 3.5 %shard_map.74 = (f32[2,8,512]{2,1,0:T(8,128)S(1)}, f32[2,8,512]{2,1,0:T(8,128)S(1)}, f32[2,128,512]{2,1,0:T(8,128)S(1)}, bf16[2,144,2048]{2,1,0:T(8,128)(2,1)S(1)}) custom-call(s32[2]{0:T(128)S(1)} %pad_add_fusion.place, s32[4]{0:T(128)S(1)} %copy-done.2, s32[4,4]{1,0:T(4,128)S(1)} %copy-done.1, bf16[64,160,128]{2,1,0:T(8,128)(2,1)S(1)} %all_to_all.10.own), custom_call_target="tpu_custom_call" | custom-call | flops 1610612736 | bytes 8388608 | tf_op jit(solution)/shard_map/pallas_call | solution.py:280
  54.8 1.1 %collective-permute-done.other = bf16[64,160,128]{2,1,0:T(8,128)(2,1)} collective-permute-done((bf16[64,160,128]{2,1,0:T(8,128)(2,1)S(1)}, bf16[64,160,128]{2,1,0:T(8,128)(2,1)}, u32[]{:S(2)}, u32[]{:S(2)}) %collective-permute-start) | collective-permute-done | bytes 2621472 | tf_op jit(solution)/shard_map/ppermute | solution.py:322
  55.9 0.0 copy-done
  55.9 0.0 copy-done.3
  55.9 10.4 %shard_map.75 = bf16[4,32,16,128]{3,2,1,0:T(8,128)(2,1)S(1)} custom-call(s32[2]{0:T(128)S(1)} %pad_add_fusion.place, s32[4]{0:T(128)S(1)} %copy-done.2, s32[4]{0:T(128)S(1)} %copy-done.3, s32[4,4]{1,0:T(4,128)S(1)} %copy-done.1, bf16[64,160,128]{2,1,0:T(8,128)(2,1)S(1)} %all_to_all.10.own, bf16[64,160,128]{2,1,0:T(8,128)(2,1)} %collective-permute-done.other, ...), custom_call_target="tpu_custom_call" | custom-call | tf_op jit(solution)/shard_map/pallas_call | solution.py:308
  66.3 17.1 %all_to_all.11 = bf16[128,16,128]{2,1,0:T(8,128)(2,1)S(1)} all-to-all(bf16[128,16,128]{2,1,0:T(8,128)(2,1)S(1)} %bitcast.10), channel_id=1, replica_groups=mesh['xh'=2,'core'=2,'ctx'=32] {'xh','core','ctx'}, dimensions={0} | all-to-all | bytes 1048576 | tf_op jit(solution)/shard_map/all_to_all | solution.py:328
  83.4 0.9 %copy.8 = bf16[4,32,16,128]{3,1,2,0:T(8,128)(2,1)} copy(bf16[4,32,16,128]{3,2,1,0:T(8,128)(2,1)S(1)} %bitcast.11) | data formatting | bytes 1048576 | tf_op jit(solution)/shard_map/reshape | solution.py:331
Async XLA Ops:
  2.7 48.6 %copy-start.1 = (s32[4,4]{1,0:T(4,128)S(1)}, s32[4,4]{1,0:T(4,128)}, u32[]{:S(2)}) copy-start(s32[4,4]{1,0:T(4,128)} %mask.3) | copy-start | bytes 196
  2.7 48.6 %copy-start.2 = (s32[4]{0:T(128)S(1)}, s32[4]{0:T(128)}, u32[]{:S(2)}) copy-start(s32[4]{0:T(128)} %order.3) | copy-start | bytes 52
  48.8 7.1 %collective-permute-start = (bf16[64,160,128]{2,1,0:T(8,128)(2,1)S(1)}, bf16[64,160,128]{2,1,0:T(8,128)(2,1)}, u32[]{:S(2)}, u32[]{:S(2)}) collective-permute-start(bf16[64,160,128]{2,1,0:T(8,128)(2,1)S(1)} %all_to_all.10.own), channel_id=1, source_target_pairs={{0,32},{32,0},{1,33},{33,1},{2,34},{34,2},{3,35},{35,3},{4,36},{36... | collective-permute-start | bytes 7864328 | tf_op jit(solution)/shard_map/ppermute | solution.py:322
  51.3 4.6 %copy-start = (f32[8,32,128]{2,1,0:T(8,128)S(1)}, f32[8,32,128]{2,1,0:T(8,128)}, u32[]{:S(2)}) copy-start(f32[8,32,128]{2,1,0:T(8,128)} %gates.1) | copy-start | bytes 393220
  51.3 4.6 %copy-start.3 = (s32[4]{0:T(128)S(1)}, s32[4]{0:T(128)}, u32[]{:S(2)}) copy-start(s32[4]{0:T(128)} %levels.1) | copy-start | bytes 52
